TPU v7x, 32 devices: a whole 2x2x4 slice. The times are simulated.
32 devices in a mesh: wide: 8 (over y, x, core), narrow: 4 (over z).
Axes of the slice: x: 2, y: 2, z: 4, core: 2. Of those that a mesh axis runs over, the one named last changes fastest.
Arguments:
- queries: bfloat16 [16384, 768], P(('wide', 'narrow')), may hold values from -150 to 150
- documents: bfloat16 [1024, 768], P(('wide', 'narrow')), may hold values from -5 to 5
- positives: int32 [16384], P(('wide', 'narrow')), may hold values from 0 to 1023
Outputs:
- losses: float32 [16384], P(('wide', 'narrow'))
- query_grad: bfloat16 [16384, 768], P(('wide', 'narrow'))
All inputs are finite; a program needn't handle non-finite values. Where the computation divides by a largest or mean magnitude, that divisor is 1e-20 or more.
Results may differ from a plain program's by a relative error of at most 0.005.
Values may be sent and summed in bfloat16 or wider, within the bound.
No kernel may reach another device: no remote copies, remote signals or barrier semaphores. Data moves between devices by JAX's collectives and lax.ppermute only.
A program may use at most 64 MiB of HBM per device.

v0:
```python
import jax
import jax.numpy as jnp
from jax import lax
from jax.sharding import PartitionSpec as P

span = 512


def block_scores(queries, codes, scales, temper):
    raw = lax.dot_general(
        queries, codes, (((1,), (1,)), ((), ())), preferred_element_type=jnp.float32
    )
    return raw * scales[None, :] * temper


def hits(positives, start, rows):
    column_ids = lax.broadcasted_iota(jnp.int32, (positives.shape[0], rows), 1) + start
    return column_ids == positives[:, None]


def sweep(update, carry, codes, scales):
    rows = codes.shape[0]

    def step(index, state):
        begin = (index * span).astype(jnp.int32)
        piece = lax.dynamic_slice_in_dim(codes, begin, span, 0)
        piece_scales = lax.dynamic_slice_in_dim(scales, begin, span, 0)
        return update(state, piece, piece_scales, begin)

    return lax.fori_loop(0, rows // span, step, carry)


def shards(queries, documents, positives):
    width = queries.shape[1]
    temper = width ** (-0.5)
    doc_values = documents.astype(jnp.float32)
    scales = jnp.max(jnp.abs(doc_values), axis=1) + 1e-06
    codes = (doc_values / scales[:, None]).astype(jnp.bfloat16)
    count = queries.shape[0]

    def totals(carry, piece, piece_scales, start):
        run_max, run_sum, chosen = carry
        scores = block_scores(queries, piece, piece_scales, temper)
        new_max = jnp.maximum(run_max, jnp.max(scores, axis=1))
        run_sum = run_sum * jnp.exp(run_max - new_max) + jnp.sum(
            jnp.exp(scores - new_max[:, None]), axis=1
        )
        found = hits(positives, start, piece.shape[0])
        chosen = chosen + jnp.sum(jnp.where(found, scores, 0.0), axis=1)
        return (new_max, run_sum, chosen)

    init = (
        jnp.full((count,), -1e30, jnp.float32),
        jnp.zeros((count,), jnp.float32),
        jnp.zeros((count,), jnp.float32),
    )
    grad_init = jnp.zeros((count, width), jnp.float32)

    def make_gradient(lse):

        def gradient(total, piece, piece_scales, start):
            scores = block_scores(queries, piece, piece_scales, temper)
            probs = jnp.exp(scores - lse[:, None])
            found = hits(positives, start, piece.shape[0]).astype(jnp.float32)
            weights = ((probs - found) * piece_scales[None, :]).astype(jnp.bfloat16)
            return total + jnp.dot(weights, piece, preferred_element_type=jnp.float32)

        return gradient

    group_codes, group_scales = (
        lax.all_gather(codes, "narrow", axis=0, tiled=True),
        lax.all_gather(scales.astype(jnp.bfloat16), "narrow", axis=0, tiled=True).astype(
            scales.dtype
        ),
    )
    pieces = (
        lax.all_gather(group_codes, "wide", axis=0, tiled=True),
        lax.all_gather(group_scales.astype(jnp.bfloat16), "wide", axis=0, tiled=True).astype(
            jnp.float32
        ),
    )
    run_max, run_sum, chosen = sweep(totals, init, pieces[0], pieces[1])
    lse = run_max + jnp.log(run_sum)
    gradient = make_gradient(lse)
    pieces = (
        lax.all_gather(group_codes, "wide", axis=0, tiled=True),
        lax.all_gather(group_scales.astype(jnp.bfloat16), "wide", axis=0, tiled=True).astype(
            jnp.float32
        ),
    )
    total = sweep(gradient, grad_init, pieces[0], pieces[1])
    losses = lse - chosen
    return (losses, (total * temper).astype(jnp.bfloat16))


def solution(mesh):
    placed = (P(("wide", "narrow"), None), P(("wide", "narrow"), None), P(("wide", "narrow")))
    return jax.shard_map(
        shards,
        mesh=mesh,
        in_specs=placed,
        out_specs=(P(("wide", "narrow")), P(("wide", "narrow"), None)),
        check_vma=False,
    )
```

profile of v0, /device:TPU:0, one launch (start us, length us, event | category | flops | bytes accessed | tf_op | source)
XLA Modules:
  0.0 72.6 jit_solution(3299232543662175232)
XLA Ops:
  7.2 0.0 all-gather.3.cloned.1.call-start
  7.2 0.9 %fusion.27 = f32[32]{0:T(128)S(1)} fusion(bf16[32,768]{1,0:T(8,128)(2,1)} %param.8), kind=kLoop, calls=%fused_computation.38 | loop fusion | flops 73696 | bytes 49280 | tf_op jit(solution)/shard_map/reduce_max | solution.py:37
  8.1 0.9 %fusion.28 = bf16[32,768]{1,0:T(8,128)(2,1)S(1)} fusion(bf16[32,768]{1,0:T(8,128)(2,1)} %param.8, f32[32]{0:T(128)S(1)} %get-tuple-element.361), kind=kLoop, calls=%fused_computation.39 | loop fusion | flops 73728 | bytes 98432 | tf_op jit(solution)/shard_map/convert_element_type | solution.py:38
  9.0 16.1 %all_gather.14 = bf16[128,768]{1,0:T(8,128)(2,1)} all-gather(bf16[32,768]{1,0:T(8,128)(2,1)S(1)} %fusion.28), channel_id=1, replica_groups=mesh['wide'=8,'narrow'=4] {'narrow'}, dimensions={0}, use_global_device_ids=true | all-gather | bytes 245760 | tf_op jit(solution)/shard_map/all_gather | solution.py:71
  25.1 0.0 all-gather.3.cloned.1.call-update
  25.2 1.2 %dynamic-slice = u32[1]{0:T(128)} dynamic-slice(u32[32]{0:T(128)} %constant.95, u32[]{:T(128)S(6)} %add.111), dynamic_slice_sizes={1} | dynamic-slice | bytes 12
  27.1 0.2 dynamic-update-slice
  27.3 12.0 %all-reduce = bf16[128]{0:T(256)(128)(2,1)S(1)} all-reduce(bf16[128]{0:T(256)(128)(2,1)S(1)} %dynamic-update-slice), channel_id=1, replica_groups=mesh['wide'=8,'narrow'=4] {'narrow'}, use_global_device_ids=true, to_apply=%add | all-reduce | flops 128 | bytes 512
  39.4 8.7 %all-gather = bf16[8,1,128]{2,1,0:T(2,128)(2,1)S(1)} all-gather(bf16[1,1,128]{2,1,0:T(2,128)(2,1)S(1)} %bitcast.33), channel_id=1, replica_groups=mesh['wide'=8,'narrow'=4] {'wide'}, dimensions={0}, use_global_device_ids=true | all-gather | bytes 2304 | tf_op jit(solution)/shard_map/all_gather | solution.py:78
  48.1 4.2 %all-gather.3.cloned.1.call-done = bf16[1024,768]{1,0:T(8,128)(2,1)} async-done(((bf16[128,768]{1,0:T(8,128)(2,1)}), bf16[1024,768]{1,0:T(8,128)(2,1)}) %all-gather.3.cloned.1.call-update) | async-done | bytes 1572880 | tf_op jit(solution)/shard_map/all_gather | solution.py:77
  52.3 4.8 %while.32 = (s32[]{:T(128)}, f32[512]{0:T(512)S(1)}, f32[512]{0:T(512)S(1)}, f32[512]{0:T(512)S(1)}, bf16[1024,768]{1,0:T(8,128)(2,1)}, /*index=5*/bf16[512,768]...) while((s32[]{:T(128)}, f32[512]{0:T(512)S(1)}, ...), condition=%wide.region_5.6_spmd.clone, body=%wide.region_1.5_spmd.clone.sunk | while | flops 404753920 | bytes 3725534 | solution.py:30
  52.3 0.0 copy-start
  52.3 0.1 dynamic_slice.45
  52.4 2.0 %fusion.41 = (f32[512]{0:T(512)S(1)}, f32[512,512]{1,0:T(8,128)S(1)}) fusion(f32[512]{0:T(512)S(1)} %dynamic_slice.45, bf16[512,768]{1,0:T(8,128)(2,1)} %get-tuple-element.495, bf16[1024,768]{1,0:T(8,128)(2,1)} %get-tuple-element.494, s32[]{:T(128)S(6)} %select_n.34), kind=kOutput, calls=%fused_computation.44.clone.1 | convolution fusion | flops 403439104 | bytes 2625540 | tf_op jit(solution)/shard_map/while/body/eval_jaxpr/dot_general | solution.py:10
  54.4 0.0 copy-done
  54.4 0.3 fusion.42
  54.7 0.0 copy-start
  54.7 0.1 dynamic_slice.45
  54.8 2.0 %fusion.41 = (f32[512]{0:T(512)S(1)}, f32[512,512]{1,0:T(8,128)S(1)}) fusion(f32[512]{0:T(512)S(1)} %dynamic_slice.45, bf16[512,768]{1,0:T(8,128)(2,1)} %get-tuple-element.495, bf16[1024,768]{1,0:T(8,128)(2,1)} %get-tuple-element.494, s32[]{:T(128)S(6)} %select_n.34), kind=kOutput, calls=%fused_computation.44.clone.1 | convolution fusion | flops 403439104 | bytes 2625540 | tf_op jit(solution)/shard_map/while/body/eval_jaxpr/dot_general | solution.py:10
  56.8 0.0 copy-done
  56.8 0.3 fusion.42
  57.1 0.6 fusion.30
  57.7 7.0 %while.33 = (s32[]{:T(128)}, f32[512,768]{1,0:T(8,128)S(1)}, bf16[1024,768]{1,0:T(8,128)(2,1)}, bf16[512,768]{1,0:T(8,128)(2,1)}, f32[1024]{0:T(1024)S(1)}, /*in...) while((s32[]{:T(128)}, f32[512,768]{1,0:T(8,128)S(1)}, ...), condition=%wide.region_7.8_spmd.clone, body=%wide.region_6.7_spmd.clone.sunk | while | flops 808190464 | bytes 5523124 | solution.py:30
  57.7 0.1 dynamic_slice.48
  57.8 3.4 %select_add_fusion.5 = f32[512,768]{1,0:T(8,128)S(1)} fusion(f32[512,768]{1,0:T(8,128)S(1)} %get-tuple-element.514, bf16[512,768]{1,0:T(8,128)(2,1)} %get-tuple-element.527, bf16[1024,768]{1,0:T(8,128)(2,1)} %get-tuple-element.526, s32[]{:T(128)S(6)} %select_n.35, pred[]{:T(512)S(6)} %compare.7, f32[512]{0:T(512)S(1)} %dynamic_slice.48, ...), kind=kOutput, calls=%fused_computation.14.clone.1 | convolution fusion | flops 808189952 | bytes 5516800 | tf_op jit(solution)/shard_map/while/body/eval_jaxpr/dot_general | solution.py:66
  61.2 0.1 dynamic_slice.48
  61.3 3.4 %select_add_fusion.5 = f32[512,768]{1,0:T(8,128)S(1)} fusion(f32[512,768]{1,0:T(8,128)S(1)} %get-tuple-element.514, bf16[512,768]{1,0:T(8,128)(2,1)} %get-tuple-element.527, bf16[1024,768]{1,0:T(8,128)(2,1)} %get-tuple-element.526, s32[]{:T(128)S(6)} %select_n.35, pred[]{:T(512)S(6)} %compare.7, f32[512]{0:T(512)S(1)} %dynamic_slice.48, ...), kind=kOutput, calls=%fused_computation.14.clone.1 | convolution fusion | flops 808189952 | bytes 5516800 | tf_op jit(solution)/shard_map/while/body/eval_jaxpr/dot_general | solution.py:66
  64.7 1.0 %multiply_convert_fusion = bf16[512,768]{1,0:T(8,128)(2,1)} fusion(f32[512,768]{1,0:T(8,128)S(1)} %get-tuple-element.270), kind=kLoop, calls=%fused_computation.35 | loop fusion | flops 786432 | bytes 2359296 | tf_op jit(solution)/shard_map/convert_element_type | solution.py:93
  (17 shorter events, 0.1 us)
Async XLA Ops:
  7.2 45.1 %all-gather.3.cloned.1.call-start = ((), (), s32[]{:S(2)}) async-start(), calls=%async_computation | async-start | bytes 1769472 | tf_op jit(solution)/shard_map/all_gather | solution.py:77
  52.3 2.1 %copy-start = (s32[512]{0:T(512)S(1)}, s32[512]{0:T(512)}, u32[]{:S(2)}) copy-start(s32[512]{0:T(512)} %get-tuple-element.497) | copy-start | bytes 6148 | tf_op jit(solution)/shard_map/while
  54.7 2.1 %copy-start = (s32[512]{0:T(512)S(1)}, s32[512]{0:T(512)}, u32[]{:S(2)}) copy-start(s32[512]{0:T(512)} %get-tuple-element.497) | copy-start | bytes 6148 | tf_op jit(solution)/shard_map/while
Sparse Core Ops, SparseCore 0:
  25.3 27.0 all-gather.2
where the time goes:
time: 73 us; the launch traced here: 72.6 us
  blocking collectives  36.8 us (50%)
  between operations  14.8 us (20%)
  matrix products  10.8 us (15%)
  waiting for transfers between devices  4.22 us (6%)
  other arithmetic  4.01 us (5%)
  local copies, waits for them, and re-layouts  1.81 us (2%)
    all_gather x1, blocking collectives, shards(): lax.all_gather(codes, 'narrow', axis=0, tiled=True)  16.1 us
    unnamed x1, blocking collectives  12 us
    all_gather x1, blocking collectives, shards(): lax.all_gather(group_scales.astype(jnp.bfloat16), 'wide', axis=0, tiled=T...  8.75 us
    dot_general x2, matrix products, gradient(): return total + jnp.dot(weights, piece, preferred_element_type=jnp.float32)  6.79 us
    all_gather x1, waiting for transfers between devices, shards(): lax.all_gather(group_codes, 'wide', axis=0, tiled=True)  4.2 us
    dot_general x2, matrix products, block_scores(): lax.dot_general(queries, codes, (((1,), (1,)), ((), ())), preferred_eleme...  3.97 us
    unnamed x3, local copies, waits for them, and re-layouts  1.49 us
  transfers between devices with their start and end apart: 1, of which 1 were waited for; matrix products, arithmetic and copies ran while one was open for 2% of the time, Pallas kernels for 0%

commit v1 on v0

v1 whole, which is shorter than its diff:
```python
import functools

import jax
import jax.numpy as jnp
from jax import lax
from jax.experimental import pallas as pl
from jax.experimental.pallas import tpu as pltpu
from jax.sharding import PartitionSpec as P

AXES = ("wide", "narrow")
NT = (((1,), (1,)), ((), ()))


def to_row(column):
    parts = []
    for start in range(0, column.shape[0], 128):
        piece = column[start : start + 128]
        size = piece.shape[0]
        r = lax.broadcasted_iota(jnp.int32, (size, size), 0)
        c = lax.broadcasted_iota(jnp.int32, (size, size), 1)
        parts.append(jnp.sum(jnp.where(r == c, piece, 0), axis=0, keepdims=True))
    return parts[0] if len(parts) == 1 else jnp.concatenate(parts, axis=1)


def kernel(n_chunks, block, spot_ref, q_ref, *refs):
    chunks = refs[:n_chunks]
    loss_ref, grad_ref, codes_ref, scales_ref, scores_ref = refs[n_chunks:]
    width = q_ref.shape[1]
    temper = width ** (-0.5)
    rows = q_ref.shape[0]
    size = chunks[0].shape[0]
    for i, chunk in enumerate(chunks):
        values = chunk[...].astype(jnp.float32)
        scale = jnp.max(jnp.abs(values), axis=1, keepdims=True) + 1e-06
        codes_ref[pl.ds(i * size, size), :] = (values / scale).astype(jnp.bfloat16)
        scales_ref[:, pl.ds(i * size, size)] = to_row(scale)
    docs = n_chunks * size
    scale_row = scales_ref[...]
    for start in range(0, rows, block):
        span = pl.ds(start, block)
        raw = lax.dot_general(
            q_ref[span, :], codes_ref[...], NT, preferred_element_type=jnp.float32
        )
        scores = raw * (scale_row * temper)
        hit = lax.broadcasted_iota(jnp.int32, (block, docs), 1) == spot_ref[span, :]
        top = jnp.max(scores, axis=1, keepdims=True)
        powers = jnp.exp(scores - top)
        total = jnp.sum(powers, axis=1, keepdims=True)
        chosen = jnp.sum(jnp.where(hit, scores, 0.0), axis=1, keepdims=True)
        loss_ref[:, span] = to_row(top + jnp.log(total) - chosen)
        probs = powers * (1.0 / total)
        weights = ((probs - jnp.where(hit, 1.0, 0.0)) * scale_row).astype(jnp.bfloat16)
        grad = jnp.dot(weights, codes_ref[...], preferred_element_type=jnp.float32)
        grad_ref[span, :] = (grad * temper).astype(jnp.bfloat16)


def shards(wide, narrow, queries, documents, positives):
    own = documents.shape[0]
    rows, width = queries.shape
    me = lax.axis_index("wide") * narrow + lax.axis_index("narrow")
    spots = (positives ^ (me * own)).reshape(rows, 1)

    def swap(array, axis, size, bits):
        return lax.ppermute(array, axis, [(i, i ^ bits) for i in range(size)])

    others = {k: swap(documents, "narrow", narrow, k) for k in reversed(range(1, narrow))}
    column = jnp.concatenate([documents] + [others[k] for k in range(1, narrow)], axis=0)
    held = {0: column}
    for k in reversed(range(2, wide, 2)):
        held[k] = swap(column, "wide", wide, k)
    for k in range(0, wide, 2):
        held[k + 1] = swap(held[k], "wide", wide, 1)
    docs = own * wide * narrow
    block = min(rows, 256)
    vmem = pl.BlockSpec(memory_space=pltpu.VMEM)
    limit = 8 * docs * width + 12 * rows * width + 12 * block * docs + 4 * 2**20
    limit = min(limit, 60 * 2**20)
    losses, grads = pl.pallas_call(
        functools.partial(kernel, wide, block),
        out_shape=(
            jax.ShapeDtypeStruct((1, rows), jnp.float32),
            jax.ShapeDtypeStruct((rows, width), jnp.bfloat16),
        ),
        in_specs=[vmem] * (2 + wide),
        out_specs=(vmem, vmem),
        scratch_shapes=[
            pltpu.VMEM((docs, width), jnp.bfloat16),
            pltpu.VMEM((1, docs), jnp.float32),
            pltpu.VMEM((8, 128), jnp.float32),
        ],
        compiler_params=pltpu.CompilerParams(vmem_limit_bytes=limit),
        cost_estimate=pl.CostEstimate(
            flops=4 * rows * docs * width,
            bytes_accessed=4 * rows * width + 2 * docs * width,
            transcendentals=rows * docs,
        ),
    )(spots, queries, *[held[k] for k in range(wide)])
    return losses.reshape(rows), grads


def solution(mesh):
    wide, narrow = mesh.shape["wide"], mesh.shape["narrow"]
    rows = P(AXES, None)
    return jax.shard_map(
        functools.partial(shards, wide, narrow),
        mesh=mesh,
        in_specs=(rows, rows, P(AXES)),
        out_specs=(P(AXES), rows),
        check_vma=False,
    )
```

time: 73 us -> 29.8 us (0.41)
  blocking collectives: 36.8 us -> 0 us
  between operations: 14.8 us -> 0.68 us
  matrix products: 10.8 us -> 0 us
  starting transfers between devices: 0.04 us -> 9.6 us
  waiting for transfers between devices: 4.22 us -> 13 us
  Pallas kernels: 0 us -> 4.14 us
  other arithmetic: 4.01 us -> 0.01 us
    all_gather x2 -> x0, blocking collectives: 24.8 us -> none  [the longest x1 16.1 us: shards(): lax.all_gather(codes, 'narrow', axis=0, tiled=True)]
    ppermute x0 -> x10, waiting for transfers between devices: none -> 13 us  [swap(): return lax.ppermute(array, axis, [(i, i ^ bits) for i in range(size)])]
    unnamed x1 -> x0, blocking collectives: 12 us -> none
    dot_general x4 -> x0, matrix products: 10.8 us -> none  [the longest x2 6.79 us: gradient(): return total + jnp.dot(weights, piece, preferred_element_type=jnp.float32)]
    ppermute x0 -> x10, starting transfers between devices: none -> 9.6 us  [swap(): return lax.ppermute(array, axis, [(i, i ^ bits) for i in range(size)])]
    all_gather x1 -> x0, waiting for transfers between devices: 4.2 us -> none  [shards(): lax.all_gather(group_codes, 'wide', axis=0, tiled=True)]
    pallas_call x0 -> x1, Pallas kernels: none -> 4.14 us  [shards(): pl.pallas_call(functools.partial(kernel, wide, block), out_shape=(jax.Sha...]
    convert_element_type x4 -> x0, other arithmetic: 1.9 us -> none  [the longest x1 1.01 us: shards(): return (losses, (total * temper).astype(jnp.bfloat16))]
  transfers between devices with their start and end apart: 1 -> 10, of which waited for: 1 -> 7; matrix products, arithmetic and copies ran while one was open for 2% -> 3% of each run, Pallas kernels for 0% -> 0%
where the time goes in v1:
time: 29.8 us; the launch traced here: 29.6 us
  waiting for transfers between devices  13 us (44%)
  starting transfers between devices  9.6 us (32%)
  Pallas kernels  4.14 us (14%)
  local copies, waits for them, and re-layouts  2.17 us (7%)
  between operations  0.68 us (2%)
    ppermute x10, waiting for transfers between devices, swap(): return lax.ppermute(array, axis, [(i, i ^ bits) for i in range(size)])  13 us
    ppermute x10, starting transfers between devices, swap(): return lax.ppermute(array, axis, [(i, i ^ bits) for i in range(size)])  9.6 us
    pallas_call x1, Pallas kernels, shards(): pl.pallas_call(functools.partial(kernel, wide, block), out_shape=(jax.Sha...  4.14 us
    unnamed x7, local copies, waits for them, and re-layouts  2.01 us
  transfers between devices with their start and end apart: 10, of which 7 were waited for; matrix products, arithmetic and copies ran while one was open for 3% of the time, Pallas kernels for 0%

profile of v1, /device:TPU:0, one launch (start us, length us, event | category | flops | bytes accessed | tf_op | source)
XLA Modules:
  0.0 29.6 jit_solution(2803669390010308883)
XLA Ops:
  0.6 4.1 %collective-permute-start.1 = (bf16[32,768]{1,0:T(8,128)(2,1)}, bf16[32,768]{1,0:T(8,128)(2,1)S(1)}, u32[]{:S(2)}, u32[]{:S(2)}) collective-permute-start(bf16[32,768]{1,0:T(8,128)(2,1)} %param.4), channel_id=1, source_target_pairs={{0,2},{1,3},{2,0},{3,1},{4,6},{5,7},{6,4},{7,5},{8,10},{9,11},{10,... | collective-permute-start | bytes 147464 | tf_op jit(solution)/shard_map/ppermute | solution.py:64
  4.7 1.6 %collective-permute-start = (bf16[32,768]{1,0:T(8,128)(2,1)}, bf16[32,768]{1,0:T(8,128)(2,1)S(1)}, u32[]{:S(2)}, u32[]{:S(2)}) collective-permute-start(bf16[32,768]{1,0:T(8,128)(2,1)} %param.4), channel_id=1, source_target_pairs={{0,1},{1,0},{2,3},{3,2},{4,5},{5,4},{6,7},{7,6},{8,9},{9,8},{10,11... | collective-permute-start | bytes 147464 | tf_op jit(solution)/shard_map/ppermute | solution.py:64
  6.3 0.0 collective-permute-start.2
  6.3 0.9 %constant_dynamic-update-slice_fusion.3 = bf16[128,768]{1,0:T(8,128)(2,1)S(1)} fusion(bf16[32,768]{1,0:T(8,128)(2,1)} %param.4), kind=kLoop, calls=%fused_computation.3 | loop fusion | bytes 98304
  7.2 1.9 %collective-permute-done = bf16[32,768]{1,0:T(8,128)(2,1)S(1)} collective-permute-done((bf16[32,768]{1,0:T(8,128)(2,1)}, bf16[32,768]{1,0:T(8,128)(2,1)S(1)}, u32[]{:S(2)}, u32[]{:S(2)}) %collective-permute-start) | collective-permute-done | bytes 49184 | tf_op jit(solution)/shard_map/ppermute | solution.py:64
  9.0 0.0 collective-permute-done.1
  9.1 3.4 %collective-permute-done.2 = bf16[32,768]{1,0:T(8,128)(2,1)S(1)} collective-permute-done((bf16[32,768]{1,0:T(8,128)(2,1)}, bf16[32,768]{1,0:T(8,128)(2,1)S(1)}, u32[]{:S(2)}, u32[]{:S(2)}) %collective-permute-start.2) | collective-permute-done | bytes 49184 | tf_op jit(solution)/shard_map/ppermute | solution.py:64
  12.4 2.4 %collective-permute-start.8 = (bf16[128,768]{1,0:T(8,128)(2,1)S(1)}, bf16[128,768]{1,0:T(8,128)(2,1)S(1)}, u32[]{:S(2)}, u32[]{:S(2)}) collective-permute-start(bf16[128,768]{1,0:T(8,128)(2,1)S(1)} %constant_dynamic-update-slice_fusion.refs_0_), channel_id=1, source_target_pairs={{0,24},{4,28},{8,16},{12,20},{16,8},{20,12},{24,0},{28,4},{1,25},{... | collective-permute-start | bytes 589832 | tf_op jit(solution)/shard_map/ppermute | solution.py:64
  14.9 0.5 %collective-permute-start.6 = (bf16[128,768]{1,0:T(8,128)(2,1)S(1)}, bf16[128,768]{1,0:T(8,128)(2,1)S(1)}, u32[]{:S(2)}, u32[]{:S(2)}) collective-permute-start(bf16[128,768]{1,0:T(8,128)(2,1)S(1)} %constant_dynamic-update-slice_fusion.refs_0_), channel_id=1, source_target_pairs={{0,16},{4,20},{8,24},{12,28},{16,0},{20,4},{24,8},{28,12},{1,17},{... | collective-permute-start | bytes 589832 | tf_op jit(solution)/shard_map/ppermute | solution.py:64
  15.4 0.5 %collective-permute-start.4 = (bf16[128,768]{1,0:T(8,128)(2,1)S(1)}, bf16[128,768]{1,0:T(8,128)(2,1)S(1)}, u32[]{:S(2)}, u32[]{:S(2)}) collective-permute-start(bf16[128,768]{1,0:T(8,128)(2,1)S(1)} %constant_dynamic-update-slice_fusion.refs_0_), channel_id=1, source_target_pairs={{0,8},{4,12},{8,0},{12,4},{16,24},{20,28},{24,16},{28,20},{1,9},{5... | collective-permute-start | bytes 589832 | tf_op jit(solution)/shard_map/ppermute | solution.py:64
  15.9 0.0 copy-start.1
  15.9 0.0 collective-permute-start.3
  15.9 5.0 %collective-permute-done.8.refs_6_ = bf16[128,768]{1,0:T(8,128)(2,1)S(1)} collective-permute-done((bf16[128,768]{1,0:T(8,128)(2,1)S(1)}, bf16[128,768]{1,0:T(8,128)(2,1)S(1)}, u32[]{:S(2)}, u32[]{:S(2)}) %collective-permute-start.8) | collective-permute-done | bytes 196640 | tf_op jit(solution)/shard_map/ppermute | solution.py:64
  20.9 0.0 collective-permute-start.9
  20.9 1.7 %collective-permute-done.6.refs_4_ = bf16[128,768]{1,0:T(8,128)(2,1)S(1)} collective-permute-done((bf16[128,768]{1,0:T(8,128)(2,1)S(1)}, bf16[128,768]{1,0:T(8,128)(2,1)S(1)}, u32[]{:S(2)}, u32[]{:S(2)}) %collective-permute-start.6) | collective-permute-done | bytes 196640 | tf_op jit(solution)/shard_map/ppermute | solution.py:64
  22.6 0.0 collective-permute-start.7
  22.6 0.1 collective-permute-done.4.refs_2_
  22.7 0.4 %collective-permute-start.5 = (bf16[128,768]{1,0:T(8,128)(2,1)S(1)}, bf16[128,768]{1,0:T(8,128)(2,1)S(1)}, u32[]{:S(2)}, u32[]{:S(2)}) collective-permute-start(bf16[128,768]{1,0:T(8,128)(2,1)S(1)} %collective-permute-done.4.refs_2_), channel_id=1, source_target_pairs={{0,4},{4,0},{8,12},{12,8},{16,20},{20,16},{24,28},{28,24},{1,5},{5... | collective-permute-start | bytes 589832 | tf_op jit(solution)/shard_map/ppermute | solution.py:64
  23.1 0.0 copy-done.1
  23.1 0.1 copy.5.spot_ref
  23.2 0.0 collective-permute-done.3.refs_1_
  23.2 0.0 collective-permute-done.9.refs_7_
  23.3 0.7 %collective-permute-done.7.refs_5_ = bf16[128,768]{1,0:T(8,128)(2,1)S(1)} collective-permute-done((bf16[128,768]{1,0:T(8,128)(2,1)S(1)}, bf16[128,768]{1,0:T(8,128)(2,1)S(1)}, u32[]{:S(2)}, u32[]{:S(2)}) %collective-permute-start.7) | collective-permute-done | bytes 196640 | tf_op jit(solution)/shard_map/ppermute | solution.py:64
  24.0 0.3 collective-permute-done.5.refs_3_
  24.3 0.0 copy-start
  24.3 1.1 %copy-done = bf16[512,768]{1,0:T(8,128)(2,1)S(1)} copy-done((bf16[512,768]{1,0:T(8,128)(2,1)S(1)}, bf16[512,768]{1,0:T(8,128)(2,1)}, u32[]{:S(2)}) %copy-start) | copy-done | bytes 786456
  25.4 4.1 %shard_map.50 = (f32[1,512]{1,0:T(1,128)}, bf16[512,768]{1,0:T(8,128)(2,1)}) custom-call(s32[512,1]{1,0:T(8,128)S(1)} %copy.5.spot_ref, bf16[512,768]{1,0:T(8,128)(2,1)S(1)} %copy-done, bf16[128,768]{1,0:T(8,128)(2,1)S(1)} %constant_dynamic-update-slice_fusion.refs_0_, bf16[128,768]{1,0:T(8,128)(2,1)S(1)} %collective-permute-done.3.refs_1_, ...), custom_call_target="tpu_custom_call" | custom-call | flops 1610612736 | bytes 3145728 | tf_op jit(solution)/shard_map/pallas_call | solution.py:78
  (4 shorter events, 0.0 us)
Async XLA Ops:
  0.6 8.4 %collective-permute-start.1 = (bf16[32,768]{1,0:T(8,128)(2,1)}, bf16[32,768]{1,0:T(8,128)(2,1)S(1)}, u32[]{:S(2)}, u32[]{:S(2)}) collective-permute-start(bf16[32,768]{1,0:T(8,128)(2,1)} %param.4), channel_id=1, source_target_pairs={{0,2},{1,3},{2,0},{3,1},{4,6},{5,7},{6,4},{7,5},{8,10},{9,11},{10,... | collective-permute-start | bytes 147464 | tf_op jit(solution)/shard_map/ppermute | solution.py:64
  4.7 4.3 %collective-permute-start = (bf16[32,768]{1,0:T(8,128)(2,1)}, bf16[32,768]{1,0:T(8,128)(2,1)S(1)}, u32[]{:S(2)}, u32[]{:S(2)}) collective-permute-start(bf16[32,768]{1,0:T(8,128)(2,1)} %param.4), channel_id=1, source_target_pairs={{0,1},{1,0},{2,3},{3,2},{4,5},{5,4},{6,7},{7,6},{8,9},{9,8},{10,11... | collective-permute-start | bytes 147464 | tf_op jit(solution)/shard_map/ppermute | solution.py:64
  6.3 6.1 %collective-permute-start.2 = (bf16[32,768]{1,0:T(8,128)(2,1)}, bf16[32,768]{1,0:T(8,128)(2,1)S(1)}, u32[]{:S(2)}, u32[]{:S(2)}) collective-permute-start(bf16[32,768]{1,0:T(8,128)(2,1)} %param.4), channel_id=1, source_target_pairs={{0,3},{1,2},{2,1},{3,0},{4,7},{5,6},{6,5},{7,4},{8,11},{9,10},{10,... | collective-permute-start | bytes 147464 | tf_op jit(solution)/shard_map/ppermute | solution.py:64
  12.4 8.5 %collective-permute-start.8 = (bf16[128,768]{1,0:T(8,128)(2,1)S(1)}, bf16[128,768]{1,0:T(8,128)(2,1)S(1)}, u32[]{:S(2)}, u32[]{:S(2)}) collective-permute-start(bf16[128,768]{1,0:T(8,128)(2,1)S(1)} %constant_dynamic-update-slice_fusion.refs_0_), channel_id=1, source_target_pairs={{0,24},{4,28},{8,16},{12,20},{16,8},{20,12},{24,0},{28,4},{1,25},{... | collective-permute-start | bytes 589832 | tf_op jit(solution)/shard_map/ppermute | solution.py:64
  14.9 7.7 %collective-permute-start.6 = (bf16[128,768]{1,0:T(8,128)(2,1)S(1)}, bf16[128,768]{1,0:T(8,128)(2,1)S(1)}, u32[]{:S(2)}, u32[]{:S(2)}) collective-permute-start(bf16[128,768]{1,0:T(8,128)(2,1)S(1)} %constant_dynamic-update-slice_fusion.refs_0_), channel_id=1, source_target_pairs={{0,16},{4,20},{8,24},{12,28},{16,0},{20,4},{24,8},{28,12},{1,17},{... | collective-permute-start | bytes 589832 | tf_op jit(solution)/shard_map/ppermute | solution.py:64
  15.4 7.3 %collective-permute-start.4 = (bf16[128,768]{1,0:T(8,128)(2,1)S(1)}, bf16[128,768]{1,0:T(8,128)(2,1)S(1)}, u32[]{:S(2)}, u32[]{:S(2)}) collective-permute-start(bf16[128,768]{1,0:T(8,128)(2,1)S(1)} %constant_dynamic-update-slice_fusion.refs_0_), channel_id=1, source_target_pairs={{0,8},{4,12},{8,0},{12,4},{16,24},{20,28},{24,16},{28,20},{1,9},{5... | collective-permute-start | bytes 589832 | tf_op jit(solution)/shard_map/ppermute | solution.py:64
  15.9 7.2 %copy-start.1 = (s32[512]{0:T(512)S(1)}, s32[512]{0:T(512)}, u32[]{:S(2)}) copy-start(s32[512]{0:T(512)} %param.5) | copy-start | bytes 6148
  15.9 7.3 %collective-permute-start.3 = (bf16[128,768]{1,0:T(8,128)(2,1)S(1)}, bf16[128,768]{1,0:T(8,128)(2,1)S(1)}, u32[]{:S(2)}, u32[]{:S(2)}) collective-permute-start(bf16[128,768]{1,0:T(8,128)(2,1)S(1)} %constant_dynamic-update-slice_fusion.refs_0_), channel_id=1, source_target_pairs={{0,4},{4,0},{8,12},{12,8},{16,20},{20,16},{24,28},{28,24},{1,5},{5... | collective-permute-start | bytes 589832 | tf_op jit(solution)/shard_map/ppermute | solution.py:64
  20.9 2.3 %collective-permute-start.9 = (bf16[128,768]{1,0:T(8,128)(2,1)S(1)}, bf16[128,768]{1,0:T(8,128)(2,1)S(1)}, u32[]{:S(2)}, u32[]{:S(2)}) collective-permute-start(bf16[128,768]{1,0:T(8,128)(2,1)S(1)} %collective-permute-done.8.refs_6_), channel_id=1, source_target_pairs={{0,4},{4,0},{8,12},{12,8},{16,20},{20,16},{24,28},{28,24},{1,5},{5... | collective-permute-start | bytes 589832 | tf_op jit(solution)/shard_map/ppermute | solution.py:64
  22.6 1.4 %collective-permute-start.7 = (bf16[128,768]{1,0:T(8,128)(2,1)S(1)}, bf16[128,768]{1,0:T(8,128)(2,1)S(1)}, u32[]{:S(2)}, u32[]{:S(2)}) collective-permute-start(bf16[128,768]{1,0:T(8,128)(2,1)S(1)} %collective-permute-done.6.refs_4_), channel_id=1, source_target_pairs={{0,4},{4,0},{8,12},{12,8},{16,20},{20,16},{24,28},{28,24},{1,5},{5... | collective-permute-start | bytes 589832 | tf_op jit(solution)/shard_map/ppermute | solution.py:64
  22.7 1.6 %collective-permute-start.5 = (bf16[128,768]{1,0:T(8,128)(2,1)S(1)}, bf16[128,768]{1,0:T(8,128)(2,1)S(1)}, u32[]{:S(2)}, u32[]{:S(2)}) collective-permute-start(bf16[128,768]{1,0:T(8,128)(2,1)S(1)} %collective-permute-done.4.refs_2_), channel_id=1, source_target_pairs={{0,4},{4,0},{8,12},{12,8},{16,20},{20,16},{24,28},{28,24},{1,5},{5... | collective-permute-start | bytes 589832 | tf_op jit(solution)/shard_map/ppermute | solution.py:64
  24.3 1.1 %copy-start = (bf16[512,768]{1,0:T(8,128)(2,1)S(1)}, bf16[512,768]{1,0:T(8,128)(2,1)}, u32[]{:S(2)}) copy-start(bf16[512,768]{1,0:T(8,128)(2,1)} %q_ref.1) | copy-start | bytes 2359300

commit v2 on v1

v2 whole, which is shorter than its diff:
```python
import functools

import jax
import jax.numpy as jnp
from jax import lax
from jax.experimental import pallas as pl
from jax.experimental.pallas import tpu as pltpu
from jax.sharding import PartitionSpec as P

AXES = ("wide", "narrow")
NT = (((1,), (1,)), ((), ()))
VMEM = pl.BlockSpec(memory_space=pltpu.VMEM)
HBM = pl.BlockSpec(memory_space=pltpu.HBM)


def to_row(column):
    parts = []
    for start in range(0, column.shape[0], 128):
        piece = column[start : start + 128]
        size = piece.shape[0]
        r = lax.broadcasted_iota(jnp.int32, (size, size), 0)
        c = lax.broadcasted_iota(jnp.int32, (size, size), 1)
        parts.append(jnp.sum(jnp.where(r == c, piece, 0), axis=0, keepdims=True))
    return parts[0] if len(parts) == 1 else jnp.concatenate(parts, axis=1)


def encode(chunks, codes_ref, scales_ref):
    group, start = [], 0
    for chunk in chunks:
        group.append(chunk[...].astype(jnp.float32))
        size = sum(part.shape[0] for part in group)
        if size % 128 and chunk is not chunks[-1]:
            continue
        values = group[0] if len(group) == 1 else jnp.concatenate(group, axis=0)
        scale = jnp.max(jnp.abs(values), axis=1, keepdims=True) + 1e-06
        codes_ref[pl.ds(start, size), :] = (values / scale).astype(jnp.bfloat16)
        scales_ref[:, pl.ds(start, size)] = to_row(scale)
        group, start = [], start + size


def ids_row(bases, own):
    rows = []
    size = max(own, 128)
    lane = lax.broadcasted_iota(jnp.int32, (1, size), 1)
    for start in range(0, len(bases), size // own):
        group = bases[start : start + size // own]
        shift = jnp.full((1, size), group[0], jnp.int32)
        for i, base in enumerate(group[1:], 1):
            shift = jnp.where(lane >= i * own, base - i * own, shift)
        rows.append((lane + shift)[:, : len(group) * own])
    return rows[0] if len(rows) == 1 else jnp.concatenate(rows, axis=1)


def softmax_part(scores, hit):
    top = jnp.max(scores, axis=1, keepdims=True)
    powers = jnp.exp(scores - top)
    total = jnp.sum(powers, axis=1, keepdims=True)
    chosen = jnp.sum(jnp.where(hit, scores, 0.0), axis=1, keepdims=True)
    return top, powers, total, chosen


def product(q, codes):
    return lax.dot_general(q, codes, NT, preferred_element_type=jnp.float32)


def load_kernel(narrow, own, positives_hbm, queries_hbm, spot_ref, q_ref, positives_ref, sem):
    fetch = pltpu.make_async_copy(positives_hbm, positives_ref, sem.at[0])
    fetch.start()
    copy = pltpu.make_async_copy(queries_hbm, q_ref, sem.at[1])
    copy.start()
    fetch.wait()
    me = lax.axis_index("wide") * narrow + lax.axis_index("narrow")
    local = (positives_ref[...] ^ (me * own)).astype(jnp.float32)
    for start in range(0, local.shape[1], 128):
        piece = local[:, start : start + 128]
        size = piece.shape[1]
        r = lax.broadcasted_iota(jnp.int32, (size, size), 0)
        c = lax.broadcasted_iota(jnp.int32, (size, size), 1)
        spot = jnp.sum(jnp.where(r == c, piece, 0.0), axis=1, keepdims=True)
        spot_ref[pl.ds(start, size), :] = spot.astype(jnp.int32)
    copy.wait()


def early_kernel(bases, own, block, spot_ref, q_ref, *refs):
    chunks = refs[:-6]
    codes_ref, scales_ref, powers_ref, top_ref, total_ref, chosen_ref = refs[-6:]
    rows, width = q_ref.shape
    temper = width ** (-0.5)
    encode(chunks, codes_ref, scales_ref)
    ids = ids_row(bases, own)
    for start in range(0, rows, block):
        span = pl.ds(start, block)
        scores = product(q_ref[span, :], codes_ref[...]) * (scales_ref[...] * temper)
        top, powers, total, chosen = softmax_part(scores, ids == spot_ref[span, :])
        powers_ref[span, :] = powers
        top_ref[span, :] = top
        total_ref[span, :] = total
        chosen_ref[span, :] = chosen


def late_kernel(bases, own, block, spot_ref, q_ref, *refs):
    states = [refs[6 * i : 6 * i + 6] for i in range(len(bases) - 1)]
    chunks = refs[6 * len(states) : -9]
    loss_hbm, grad_hbm, codes_ref, late_scales_ref, weights_ref, loss_ref, grad_ref, sem, loss_sem = refs[-9:]
    rows, width = q_ref.shape
    temper = width ** (-0.5)
    n_late = len(bases[-1]) * own
    n_early = codes_ref.shape[0] - n_late
    late_codes_ref = codes_ref.at[pl.ds(n_early, n_late), :]
    encode(chunks, late_codes_ref, late_scales_ref)
    places = []
    for state in states:
        size = state[0].shape[0]
        places.append(pl.ds(sum(place.size for place in places), size))
        codes_ref[places[-1], :] = state[0][...]
    late_scales = late_scales_ref[...]
    ids = [ids_row(part, own) for part in bases]

    def weigh(start):
        span = pl.ds(start, block)
        spots = spot_ref[span, :]
        scores = product(q_ref[span, :], late_codes_ref[...]) * (late_scales * temper)
        late_hit = ids[-1] == spots
        late_top, late_powers, late_total, chosen = softmax_part(scores, late_hit)
        top = late_top
        for state in states:
            top = jnp.maximum(top, state[3][span, :])
        late_share = jnp.exp(late_top - top)
        shares = [jnp.exp(state[3][span, :] - top) for state in states]
        total = late_total * late_share
        for state, share in zip(states, shares):
            total += state[4][span, :] * share
            chosen += state[5][span, :]
        loss_ref[:, span] = to_row(top + jnp.log(total) - chosen)
        for state, share, place, part in zip(states, shares, places, ids):
            probs = state[2][span, :] * (share / total)
            weights = (probs - jnp.where(part == spots, 1.0, 0.0)) * state[1][...]
            weights_ref[span, place] = weights.astype(jnp.bfloat16)
        probs = late_powers * (late_share / total)
        weights = (probs - jnp.where(late_hit, 1.0, 0.0)) * late_scales
        weights_ref[span, pl.ds(n_early, n_late)] = weights.astype(jnp.bfloat16)

    starts = range(0, rows, block)
    for start in starts:
        weigh(start)
    copies = [pltpu.make_async_copy(loss_ref, loss_hbm, loss_sem)]
    copies[0].start()
    for i, start in enumerate(starts):
        span = pl.ds(start, block)
        grad = jnp.dot(weights_ref[span, :], codes_ref[...], preferred_element_type=jnp.float32)
        grad_ref[span, :] = (grad * temper).astype(jnp.bfloat16)
        copy = pltpu.make_async_copy(grad_ref.at[span, :], grad_hbm.at[span, :], sem.at[i])
        copy.start()
        copies.append(copy)
    for copy in copies:
        copy.wait()


def shards(wide, narrow, queries, documents, positives):
    own = documents.shape[0]
    rows, width = queries.shape
    f32, bf16 = jnp.float32, jnp.bfloat16
    barrier = lax.optimization_barrier
    block = min(rows, 256)
    far = range(2, wide, 2)

    def swap(array, axis, bits):
        size = wide if axis == "wide" else narrow
        return lax.ppermute(array, axis, [(i, i ^ bits) for i in range(size)])

    def params(docs, kept):
        held = 6 * docs * width + 8 * rows * width + 4 * rows * (kept + 512) + 12 * block * docs
        return dict(
            compiler_params=pltpu.CompilerParams(
                vmem_limit_bytes=min(held + 4 * 2**20, 60 * 2**20)
            ),
            cost_estimate=pl.CostEstimate(flops=rows, bytes_accessed=rows, transcendentals=0),
        )

    def load(positives, queries):
        return pl.pallas_call(
            functools.partial(load_kernel, narrow, own),
            out_shape=(
                jax.ShapeDtypeStruct((rows, 1), jnp.int32),
                jax.ShapeDtypeStruct((rows, width), bf16),
            ),
            in_specs=[HBM, HBM],
            out_specs=(VMEM, VMEM),
            scratch_shapes=[pltpu.VMEM((1, rows), jnp.int32), pltpu.SemaphoreType.DMA((2,))],
            **params(0, 0),
        )(positives.reshape(1, rows), queries)

    def bases_of(distances):
        return [(k * narrow + n) * own for k in distances for n in range(narrow)]

    def score(spots, loaded, distances, chunks):
        docs = len(chunks) * own * narrow
        column = jax.ShapeDtypeStruct((rows, 1), f32)
        return pl.pallas_call(
            functools.partial(early_kernel, bases_of(distances), own, block),
            out_shape=(
                jax.ShapeDtypeStruct((docs, width), bf16),
                jax.ShapeDtypeStruct((1, docs), f32),
                jax.ShapeDtypeStruct((rows, docs), f32),
                column,
                column,
                column,
            ),
            in_specs=[VMEM] * (2 + len(chunks)),
            out_specs=(VMEM,) * 6,
            **params(docs, docs),
        )(spots, loaded, *chunks)

    shard = {k: swap(documents, "narrow", k) for k in reversed(range(1, narrow))}
    column = jnp.concatenate([documents] + [shard[k] for k in range(1, narrow)], axis=0)
    held = {k: swap(column, "wide", k) for k in reversed(far)}
    column, positives, queries = barrier((column, positives, queries))
    spots, loaded = load(positives, queries)
    held[0] = column
    spots, loaded, held = barrier((spots, loaded, held))
    mine = range(0, wide, 2)
    middle = score(spots, loaded, mine, [held[k] for k in mine])
    mirrored = [swap(held[k], "wide", 1) for k in mine]
    docs = own * narrow * wide
    bases = [bases_of(mine), bases_of([k ^ 1 for k in mine])]
    n_late = len(bases[-1]) * own
    losses, grads = pl.pallas_call(
        functools.partial(late_kernel, bases, own, block),
        out_shape=(
            jax.ShapeDtypeStruct((1, rows), f32),
            jax.ShapeDtypeStruct((rows, width), bf16),
        ),
        in_specs=[VMEM] * (2 + len(middle) + len(mirrored)),
        out_specs=(HBM, HBM),
        scratch_shapes=[
            pltpu.VMEM((docs, width), bf16),
            pltpu.VMEM((1, n_late), f32),
            pltpu.VMEM((rows, docs), bf16),
            pltpu.VMEM((1, rows), f32),
            pltpu.VMEM((rows, width), bf16),
            pltpu.SemaphoreType.DMA((rows // block,)),
            pltpu.SemaphoreType.DMA(()),
        ],
        **params(docs, docs),
    )(spots, loaded, *middle, *mirrored)
    return losses.reshape(rows), grads


def solution(mesh):
    wide, narrow = mesh.shape["wide"], mesh.shape["narrow"]
    rows = P(AXES, None)
    return jax.shard_map(
        functools.partial(shards, wide, narrow),
        mesh=mesh,
        in_specs=(rows, rows, P(AXES)),
        out_specs=(P(AXES), rows),
        check_vma=False,
    )
```

time: 29.8 us -> 28 us (0.940)
  waiting for transfers between devices: 13 us -> 10.8 us
  starting transfers between devices: 9.6 us -> 10.2 us
    ppermute x10, waiting for transfers between devices: 13 us -> 10.8 us  [swap(): return lax.ppermute(array, axis, [(i, i ^ bits) for i in range(size)])]
    ppermute x10, starting transfers between devices: 9.6 us -> 10.2 us  [swap(): return lax.ppermute(array, axis, [(i, i ^ bits) for i in range(size)])]
    pallas_call x1 -> x3, Pallas kernels: 4.14 us -> 4.03 us  [the longest x1 2.8 us: shards(): pl.pallas_call(functools.partial(late_kernel, bases, own, block), out_sha...]
  transfers between devices with their start and end apart: 10 -> 10, of which waited for: 7 -> 6; matrix products, arithmetic and copies ran while one was open for 3% -> 3% of each run, Pallas kernels for 0% -> 4%
where the time goes in v2:
time: 28 us; the launch traced here: 27.8 us
  waiting for transfers between devices  10.8 us (39%)
  starting transfers between devices  10.2 us (36%)
  Pallas kernels  4.03 us (14%)
  local copies, waits for them, and re-layouts  2.02 us (7%)
  between operations  0.68 us (2%)
    ppermute x10, waiting for transfers between devices, swap(): return lax.ppermute(array, axis, [(i, i ^ bits) for i in range(size)])  10.8 us
    ppermute x10, starting transfers between devices, swap(): return lax.ppermute(array, axis, [(i, i ^ bits) for i in range(size)])  10.2 us
    pallas_call x1, Pallas kernels, shards(): pl.pallas_call(functools.partial(late_kernel, bases, own, block), out_sha...  2.8 us
    unnamed x7, local copies, waits for them, and re-layouts  2.01 us
    pallas_call x1, Pallas kernels, score(): pl.pallas_call(functools.partial(early_kernel, bases_of(distances), own,...  1 us
  transfers between devices with their start and end apart: 10, of which 6 were waited for; matrix products, arithmetic and copies ran while one was open for 3% of the time, Pallas kernels for 4%

profile of v2, /device:TPU:0, one launch (start us, length us, event | category | flops | bytes accessed | tf_op | source)
XLA Modules:
  0.0 27.8 jit_solution(12806132519238938655)
XLA Ops:
  0.6 4.1 %collective-permute-start.1 = (bf16[32,768]{1,0:T(8,128)(2,1)}, bf16[32,768]{1,0:T(8,128)(2,1)S(1)}, u32[]{:S(2)}, u32[]{:S(2)}) collective-permute-start(bf16[32,768]{1,0:T(8,128)(2,1)} %param.4), channel_id=1, source_target_pairs={{0,2},{1,3},{2,0},{3,1},{4,6},{5,7},{6,4},{7,5},{8,10},{9,11},{10,... | collective-permute-start | bytes 147464 | tf_op jit(solution)/shard_map/ppermute | solution.py:169
  4.7 1.6 %collective-permute-start = (bf16[32,768]{1,0:T(8,128)(2,1)}, bf16[32,768]{1,0:T(8,128)(2,1)S(1)}, u32[]{:S(2)}, u32[]{:S(2)}) collective-permute-start(bf16[32,768]{1,0:T(8,128)(2,1)} %param.4), channel_id=1, source_target_pairs={{0,1},{1,0},{2,3},{3,2},{4,5},{5,4},{6,7},{7,6},{8,9},{9,8},{10,11... | collective-permute-start | bytes 147464 | tf_op jit(solution)/shard_map/ppermute | solution.py:169
  6.3 0.0 collective-permute-start.2
  6.3 0.9 %constant_dynamic-update-slice_fusion.3 = bf16[128,768]{1,0:T(8,128)(2,1)S(1)} fusion(bf16[32,768]{1,0:T(8,128)(2,1)} %param.4), kind=kLoop, calls=%fused_computation.3 | loop fusion | bytes 98304
  7.2 1.9 %collective-permute-done = bf16[32,768]{1,0:T(8,128)(2,1)S(1)} collective-permute-done((bf16[32,768]{1,0:T(8,128)(2,1)}, bf16[32,768]{1,0:T(8,128)(2,1)S(1)}, u32[]{:S(2)}, u32[]{:S(2)}) %collective-permute-start) | collective-permute-done | bytes 49184 | tf_op jit(solution)/shard_map/ppermute | solution.py:169
  9.0 0.0 collective-permute-done.1
  9.1 3.4 %collective-permute-done.2 = bf16[32,768]{1,0:T(8,128)(2,1)S(1)} collective-permute-done((bf16[32,768]{1,0:T(8,128)(2,1)}, bf16[32,768]{1,0:T(8,128)(2,1)S(1)}, u32[]{:S(2)}, u32[]{:S(2)}) %collective-permute-start.2) | collective-permute-done | bytes 49184 | tf_op jit(solution)/shard_map/ppermute | solution.py:169
  12.4 0.0 copy-start.1
  12.4 2.4 %collective-permute-start.5 = (bf16[128,768]{1,0:T(8,128)(2,1)S(1)}, bf16[128,768]{1,0:T(8,128)(2,1)S(1)}, u32[]{:S(2)}, u32[]{:S(2)}) collective-permute-start(bf16[128,768]{1,0:T(8,128)(2,1)S(1)} %constant_dynamic-update-slice_fusion.refs_0_), channel_id=1, source_target_pairs={{0,24},{4,28},{8,16},{12,20},{16,8},{20,12},{24,0},{28,4},{1,25},{... | collective-permute-start | bytes 589832 | tf_op jit(solution)/shard_map/ppermute | solution.py:169
  14.9 0.5 %collective-permute-start.4 = (bf16[128,768]{1,0:T(8,128)(2,1)S(1)}, bf16[128,768]{1,0:T(8,128)(2,1)S(1)}, u32[]{:S(2)}, u32[]{:S(2)}) collective-permute-start(bf16[128,768]{1,0:T(8,128)(2,1)S(1)} %constant_dynamic-update-slice_fusion.refs_0_), channel_id=1, source_target_pairs={{0,16},{4,20},{8,24},{12,28},{16,0},{20,4},{24,8},{28,12},{1,17},{... | collective-permute-start | bytes 589832 | tf_op jit(solution)/shard_map/ppermute | solution.py:169
  15.4 0.5 %collective-permute-start.3 = (bf16[128,768]{1,0:T(8,128)(2,1)S(1)}, bf16[128,768]{1,0:T(8,128)(2,1)S(1)}, u32[]{:S(2)}, u32[]{:S(2)}) collective-permute-start(bf16[128,768]{1,0:T(8,128)(2,1)S(1)} %constant_dynamic-update-slice_fusion.refs_0_), channel_id=1, source_target_pairs={{0,8},{4,12},{8,0},{12,4},{16,24},{20,28},{24,16},{28,20},{1,9},{5... | collective-permute-start | bytes 589832 | tf_op jit(solution)/shard_map/ppermute | solution.py:169
  15.9 0.0 copy-done.1
  15.9 0.0 copy-start
  15.9 1.1 %copy-done = bf16[512,768]{1,0:T(8,128)(2,1)S(1)} copy-done((bf16[512,768]{1,0:T(8,128)(2,1)S(1)}, bf16[512,768]{1,0:T(8,128)(2,1)}, u32[]{:S(2)}) %copy-start) | copy-done | bytes 786456
  17.0 0.2 shard_map.50
  17.3 3.6 %collective-permute-done.5.refs_3_ = bf16[128,768]{1,0:T(8,128)(2,1)S(1)} collective-permute-done((bf16[128,768]{1,0:T(8,128)(2,1)S(1)}, bf16[128,768]{1,0:T(8,128)(2,1)S(1)}, u32[]{:S(2)}, u32[]{:S(2)}) %collective-permute-start.5) | collective-permute-done | bytes 196640 | tf_op jit(solution)/shard_map/ppermute | solution.py:169
  20.9 1.7 %collective-permute-done.4.refs_2_ = bf16[128,768]{1,0:T(8,128)(2,1)S(1)} collective-permute-done((bf16[128,768]{1,0:T(8,128)(2,1)S(1)}, bf16[128,768]{1,0:T(8,128)(2,1)S(1)}, u32[]{:S(2)}, u32[]{:S(2)}) %collective-permute-start.4) | collective-permute-done | bytes 196640 | tf_op jit(solution)/shard_map/ppermute | solution.py:169
  22.6 0.1 collective-permute-done.3.refs_1_
  22.7 0.0 collective-permute-start.6
  22.7 0.5 %collective-permute-start.7 = (bf16[128,768]{1,0:T(8,128)(2,1)S(1)}, bf16[128,768]{1,0:T(8,128)(2,1)S(1)}, u32[]{:S(2)}, u32[]{:S(2)}) collective-permute-start(bf16[128,768]{1,0:T(8,128)(2,1)S(1)} %collective-permute-done.3.refs_1_), channel_id=1, source_target_pairs={{0,4},{4,0},{8,12},{12,8},{16,20},{20,16},{24,28},{28,24},{1,5},{5... | collective-permute-start | bytes 589832 | tf_op jit(solution)/shard_map/ppermute | solution.py:169
  23.2 0.0 collective-permute-start.8
  23.2 0.5 %collective-permute-start.9 = (bf16[128,768]{1,0:T(8,128)(2,1)S(1)}, bf16[128,768]{1,0:T(8,128)(2,1)S(1)}, u32[]{:S(2)}, u32[]{:S(2)}) collective-permute-start(bf16[128,768]{1,0:T(8,128)(2,1)S(1)} %collective-permute-done.5.refs_3_), channel_id=1, source_target_pairs={{0,4},{4,0},{8,12},{12,8},{16,20},{20,16},{24,28},{28,24},{1,5},{5... | collective-permute-start | bytes 589832 | tf_op jit(solution)/shard_map/ppermute | solution.py:169
  23.7 1.0 %shard_map.51 = (bf16[512,768]{1,0:T(8,128)(2,1)S(1)}, f32[1,512]{1,0:T(1,128)S(1)}, f32[512,512]{1,0:T(8,128)S(1)}, f32[512,1]{1,0:T(8,128)S(1)}, f32[512,1]{1,0:T(8,128)S(1)}, /*index=5*/f32[512,1]{1,0:T(8,128)S(1)}) custom-call(s32[512,1]{1,0:T(8,128)S(1)} %get-tuple-element.26.spot_ref, bf16[512,768]{1,0:T(8,128)(2,1)S(1)} %get-tuple-element.27.q_ref, ...), custom_call_target="tpu_custom_call" | custom-call | flops 512 | bytes 512 | tf_op jit(solution)/shard_map/pallas_call | solution.py:199
  24.7 0.0 collective-permute-done.6.refs_6_
  24.7 0.0 collective-permute-done.7.refs_7_
  24.7 0.0 collective-permute-done.8.refs_8_
  24.7 0.2 collective-permute-done.9.refs_9_
  24.9 2.8 %shard_map.52 = (f32[1,512]{1,0:T(1,128)}, bf16[512,768]{1,0:T(8,128)(2,1)}) custom-call(s32[512,1]{1,0:T(8,128)S(1)} %get-tuple-element.26.spot_ref, bf16[512,768]{1,0:T(8,128)(2,1)S(1)} %get-tuple-element.27.q_ref, bf16[512,768]{1,0:T(8,128)(2,1)S(1)} %get-tuple-element.32.refs_0_, f32[1,512]{1,0:T(1,128)S(1)} %get-tuple-element.33.refs_1_, ...), custom_call_target="tpu_custom_call" | custom-call | flops 512 | bytes 512 | tf_op jit(solution)/shard_map/pallas_call | solution.py:227
  (3 shorter events, 0.0 us)
Async XLA Ops:
  0.6 8.4 %collective-permute-start.1 = (bf16[32,768]{1,0:T(8,128)(2,1)}, bf16[32,768]{1,0:T(8,128)(2,1)S(1)}, u32[]{:S(2)}, u32[]{:S(2)}) collective-permute-start(bf16[32,768]{1,0:T(8,128)(2,1)} %param.4), channel_id=1, source_target_pairs={{0,2},{1,3},{2,0},{3,1},{4,6},{5,7},{6,4},{7,5},{8,10},{9,11},{10,... | collective-permute-start | bytes 147464 | tf_op jit(solution)/shard_map/ppermute | solution.py:169
  4.7 4.3 %collective-permute-start = (bf16[32,768]{1,0:T(8,128)(2,1)}, bf16[32,768]{1,0:T(8,128)(2,1)S(1)}, u32[]{:S(2)}, u32[]{:S(2)}) collective-permute-start(bf16[32,768]{1,0:T(8,128)(2,1)} %param.4), channel_id=1, source_target_pairs={{0,1},{1,0},{2,3},{3,2},{4,5},{5,4},{6,7},{7,6},{8,9},{9,8},{10,11... | collective-permute-start | bytes 147464 | tf_op jit(solution)/shard_map/ppermute | solution.py:169
  6.3 6.1 %collective-permute-start.2 = (bf16[32,768]{1,0:T(8,128)(2,1)}, bf16[32,768]{1,0:T(8,128)(2,1)S(1)}, u32[]{:S(2)}, u32[]{:S(2)}) collective-permute-start(bf16[32,768]{1,0:T(8,128)(2,1)} %param.4), channel_id=1, source_target_pairs={{0,3},{1,2},{2,1},{3,0},{4,7},{5,6},{6,5},{7,4},{8,11},{9,10},{10,... | collective-permute-start | bytes 147464 | tf_op jit(solution)/shard_map/ppermute | solution.py:169
  12.4 3.5 %copy-start.1 = (s32[512]{0:T(512)S(1)}, s32[512]{0:T(512)}, u32[]{:S(2)}) copy-start(s32[512]{0:T(512)} %param.5) | copy-start | bytes 6148
  12.4 8.5 %collective-permute-start.5 = (bf16[128,768]{1,0:T(8,128)(2,1)S(1)}, bf16[128,768]{1,0:T(8,128)(2,1)S(1)}, u32[]{:S(2)}, u32[]{:S(2)}) collective-permute-start(bf16[128,768]{1,0:T(8,128)(2,1)S(1)} %constant_dynamic-update-slice_fusion.refs_0_), channel_id=1, source_target_pairs={{0,24},{4,28},{8,16},{12,20},{16,8},{20,12},{24,0},{28,4},{1,25},{... | collective-permute-start | bytes 589832 | tf_op jit(solution)/shard_map/ppermute | solution.py:169
  14.9 7.7 %collective-permute-start.4 = (bf16[128,768]{1,0:T(8,128)(2,1)S(1)}, bf16[128,768]{1,0:T(8,128)(2,1)S(1)}, u32[]{:S(2)}, u32[]{:S(2)}) collective-permute-start(bf16[128,768]{1,0:T(8,128)(2,1)S(1)} %constant_dynamic-update-slice_fusion.refs_0_), channel_id=1, source_target_pairs={{0,16},{4,20},{8,24},{12,28},{16,0},{20,4},{24,8},{28,12},{1,17},{... | collective-permute-start | bytes 589832 | tf_op jit(solution)/shard_map/ppermute | solution.py:169
  15.4 7.3 %collective-permute-start.3 = (bf16[128,768]{1,0:T(8,128)(2,1)S(1)}, bf16[128,768]{1,0:T(8,128)(2,1)S(1)}, u32[]{:S(2)}, u32[]{:S(2)}) collective-permute-start(bf16[128,768]{1,0:T(8,128)(2,1)S(1)} %constant_dynamic-update-slice_fusion.refs_0_), channel_id=1, source_target_pairs={{0,8},{4,12},{8,0},{12,4},{16,24},{20,28},{24,16},{28,20},{1,9},{5... | collective-permute-start | bytes 589832 | tf_op jit(solution)/shard_map/ppermute | solution.py:169
  15.9 1.1 %copy-start = (bf16[512,768]{1,0:T(8,128)(2,1)S(1)}, bf16[512,768]{1,0:T(8,128)(2,1)}, u32[]{:S(2)}) copy-start(bf16[512,768]{1,0:T(8,128)(2,1)} %queries_hbm) | copy-start | bytes 2359300
  22.7 2.0 %collective-permute-start.6 = (bf16[128,768]{1,0:T(8,128)(2,1)S(1)}, bf16[128,768]{1,0:T(8,128)(2,1)S(1)}, u32[]{:S(2)}, u32[]{:S(2)}) collective-permute-start(bf16[128,768]{1,0:T(8,128)(2,1)S(1)} %constant_dynamic-update-slice_fusion.refs_0_), channel_id=1, source_target_pairs={{0,4},{4,0},{8,12},{12,8},{16,20},{20,16},{24,28},{28,24},{1,5},{5... | collective-permute-start | bytes 589832 | tf_op jit(solution)/shard_map/ppermute | solution.py:169
  22.7 2.0 %collective-permute-start.7 = (bf16[128,768]{1,0:T(8,128)(2,1)S(1)}, bf16[128,768]{1,0:T(8,128)(2,1)S(1)}, u32[]{:S(2)}, u32[]{:S(2)}) collective-permute-start(bf16[128,768]{1,0:T(8,128)(2,1)S(1)} %collective-permute-done.3.refs_1_), channel_id=1, source_target_pairs={{0,4},{4,0},{8,12},{12,8},{16,20},{20,16},{24,28},{28,24},{1,5},{5... | collective-permute-start | bytes 589832 | tf_op jit(solution)/shard_map/ppermute | solution.py:169
  23.2 1.5 %collective-permute-start.8 = (bf16[128,768]{1,0:T(8,128)(2,1)S(1)}, bf16[128,768]{1,0:T(8,128)(2,1)S(1)}, u32[]{:S(2)}, u32[]{:S(2)}) collective-permute-start(bf16[128,768]{1,0:T(8,128)(2,1)S(1)} %collective-permute-done.4.refs_2_), channel_id=1, source_target_pairs={{0,4},{4,0},{8,12},{12,8},{16,20},{20,16},{24,28},{28,24},{1,5},{5... | collective-permute-start | bytes 589832 | tf_op jit(solution)/shard_map/ppermute | solution.py:169
  23.2 1.8 %collective-permute-start.9 = (bf16[128,768]{1,0:T(8,128)(2,1)S(1)}, bf16[128,768]{1,0:T(8,128)(2,1)S(1)}, u32[]{:S(2)}, u32[]{:S(2)}) collective-permute-start(bf16[128,768]{1,0:T(8,128)(2,1)S(1)} %collective-permute-done.5.refs_3_), channel_id=1, source_target_pairs={{0,4},{4,0},{8,12},{12,8},{16,20},{20,16},{24,28},{28,24},{1,5},{5... | collective-permute-start | bytes 589832 | tf_op jit(solution)/shard_map/ppermute | solution.py:169

commit v3 on v2

--- a/solution.py
+++ b/solution.py
@@ -163,6 +163,8 @@
     barrier = lax.optimization_barrier
     block = min(rows, 256)
     far = range(2, wide, 2)
+    evens = list(range(0, narrow, 2))
+    order = evens + [k ^ 1 for k in evens]
 
     def swap(array, axis, bits):
         size = wide if axis == "wide" else narrow
@@ -191,10 +193,10 @@
         )(positives.reshape(1, rows), queries)
 
     def bases_of(distances):
-        return [(k * narrow + n) * own for k in distances for n in range(narrow)]
+        return [(k * narrow + n) * own for k in distances for n in order]
 
     def score(spots, loaded, distances, chunks):
-        docs = len(chunks) * own * narrow
+        docs = len(distances) * own * narrow
         column = jax.ShapeDtypeStruct((rows, 1), f32)
         return pl.pallas_call(
             functools.partial(early_kernel, bases_of(distances), own, block),
@@ -211,16 +213,24 @@
             **params(docs, docs),
         )(spots, loaded, *chunks)
 
-    shard = {k: swap(documents, "narrow", k) for k in reversed(range(1, narrow))}
-    column = jnp.concatenate([documents] + [shard[k] for k in range(1, narrow)], axis=0)
-    held = {k: swap(column, "wide", k) for k in reversed(far)}
+    shard = {0: documents} | {k: swap(documents, "narrow", k) for k in evens[1:]}
+    base = jnp.concatenate([shard[k] for k in evens], axis=0)
+    firsts = {k: swap(base, "wide", k) for k in far if k & (k - 1)}
+    other = swap(base, "narrow", 1)
+    column = jnp.concatenate([base, other], axis=0)
+    held = {}
+    for k in far:
+        if k & (k - 1) == 0:
+            held[k] = [swap(column, "wide", k)]
+        else:
+            held[k] = [firsts[k], swap(firsts[k], "narrow", 1)]
     column, positives, queries = barrier((column, positives, queries))
     spots, loaded = load(positives, queries)
-    held[0] = column
+    held[0] = [column]
     spots, loaded, held = barrier((spots, loaded, held))
     mine = range(0, wide, 2)
-    middle = score(spots, loaded, mine, [held[k] for k in mine])
-    mirrored = [swap(held[k], "wide", 1) for k in mine]
+    middle = score(spots, loaded, mine, [part for k in mine for part in held[k]])
+    mirrored = [swap(part, "wide", 1) for k in mine for part in held[k]]
     docs = own * narrow * wide
     bases = [bases_of(mine), bases_of([k ^ 1 for k in mine])]
     n_late = len(bases[-1]) * own

time: 28 us -> 25.5 us (0.911)
  waiting for transfers between devices: 10.8 us -> 5.11 us
  starting transfers between devices: 10.2 us -> 13.5 us
    ppermute x10 -> x11, waiting for transfers between devices: 10.8 us -> 5.11 us  [swap(): return lax.ppermute(array, axis, [(i, i ^ bits) for i in range(size)])]
    ppermute x10 -> x11, starting transfers between devices: 10.2 us -> 13.5 us  [swap(): return lax.ppermute(array, axis, [(i, i ^ bits) for i in range(size)])]
    unnamed x7 -> x5, local copies, waits for them, and re-layouts: 2.01 us -> 1.98 us
  transfers between devices with their start and end apart: 10 -> 11, of which waited for: 6 -> 5; matrix products, arithmetic and copies ran while one was open for 3% -> 3% of each run, Pallas kernels for 4% -> 5%
where the time goes in v3:
time: 25.5 us; the launch traced here: 25.3 us
  starting transfers between devices  13.5 us (53%)
  waiting for transfers between devices  5.11 us (20%)
  Pallas kernels  4.05 us (16%)
  local copies, waits for them, and re-layouts  1.99 us (8%)
  between operations  0.67 us (3%)
    ppermute x11, starting transfers between devices, swap(): return lax.ppermute(array, axis, [(i, i ^ bits) for i in range(size)])  13.5 us
    ppermute x11, waiting for transfers between devices, swap(): return lax.ppermute(array, axis, [(i, i ^ bits) for i in range(size)])  5.11 us
    pallas_call x1, Pallas kernels, shards(): pl.pallas_call(functools.partial(late_kernel, bases, own, block), out_sha...  2.82 us
    unnamed x5, local copies, waits for them, and re-layouts  1.98 us
    pallas_call x1, Pallas kernels, score(): pl.pallas_call(functools.partial(early_kernel, bases_of(distances), own,...  1 us
  transfers between devices with their start and end apart: 11, of which 5 were waited for; matrix products, arithmetic and copies ran while one was open for 3% of the time, Pallas kernels for 5%

profile of v3, /device:TPU:0, one launch (start us, length us, event | category | flops | bytes accessed | tf_op | source)
XLA Modules:
  0.0 25.3 jit_solution(10073569544533179323)
XLA Ops:
  0.6 4.1 %collective-permute-start = (bf16[32,768]{1,0:T(8,128)(2,1)}, bf16[32,768]{1,0:T(8,128)(2,1)S(1)}, u32[]{:S(2)}, u32[]{:S(2)}) collective-permute-start(bf16[32,768]{1,0:T(8,128)(2,1)} %param.4), channel_id=1, source_target_pairs={{0,2},{1,3},{2,0},{3,1},{4,6},{5,7},{6,4},{7,5},{8,10},{9,11},{10,... | collective-permute-start | bytes 147464 | tf_op jit(solution)/shard_map/ppermute | solution.py:171
  4.7 0.8 %constant_dynamic-update-slice_fusion.1 = (bf16[64,768]{1,0:T(8,128)(2,1)S(1)}, bf16[128,768]{1,0:T(8,128)(2,1)S(1)}) fusion(bf16[32,768]{1,0:T(8,128)(2,1)} %param.4), kind=kLoop, calls=%fused_computation.1 | loop fusion | bytes 147456
  5.6 2.0 %collective-permute-done = bf16[32,768]{1,0:T(8,128)(2,1)S(1)} collective-permute-done((bf16[32,768]{1,0:T(8,128)(2,1)}, bf16[32,768]{1,0:T(8,128)(2,1)S(1)}, u32[]{:S(2)}, u32[]{:S(2)}) %collective-permute-start) | collective-permute-done | bytes 49184 | tf_op jit(solution)/shard_map/ppermute | solution.py:171
  7.5 1.4 %collective-permute-start.1 = (bf16[64,768]{1,0:T(8,128)(2,1)S(1)}, bf16[64,768]{1,0:T(8,128)(2,1)S(1)}, u32[]{:S(2)}, u32[]{:S(2)}) collective-permute-start(bf16[64,768]{1,0:T(8,128)(2,1)S(1)} %get-tuple-element.42), channel_id=1, source_target_pairs={{0,1},{1,0},{2,3},{3,2},{4,5},{5,4},{6,7},{7,6},{8,9},{9,8},{10,11... | collective-permute-start | bytes 294920 | tf_op jit(solution)/shard_map/ppermute | solution.py:171
  9.0 2.4 %collective-permute-start.4 = (bf16[64,768]{1,0:T(8,128)(2,1)S(1)}, bf16[64,768]{1,0:T(8,128)(2,1)S(1)}, u32[]{:S(2)}, u32[]{:S(2)}) collective-permute-start(bf16[64,768]{1,0:T(8,128)(2,1)S(1)} %get-tuple-element.42), channel_id=1, source_target_pairs={{0,24},{4,28},{8,16},{12,20},{16,8},{20,12},{24,0},{28,4},{1,25},{... | collective-permute-start | bytes 294920 | tf_op jit(solution)/shard_map/ppermute | solution.py:171
  11.4 0.8 %collective-permute-done.1 = bf16[64,768]{1,0:T(8,128)(2,1)S(1)} collective-permute-done((bf16[64,768]{1,0:T(8,128)(2,1)S(1)}, bf16[64,768]{1,0:T(8,128)(2,1)S(1)}, u32[]{:S(2)}, u32[]{:S(2)}) %collective-permute-start.1) | collective-permute-done | bytes 98336 | tf_op jit(solution)/shard_map/ppermute | solution.py:171
  12.2 0.0 copy-start.1
  12.2 1.8 %collective-permute-start.3 = (bf16[128,768]{1,0:T(8,128)(2,1)S(1)}, bf16[128,768]{1,0:T(8,128)(2,1)S(1)}, u32[]{:S(2)}, u32[]{:S(2)}) collective-permute-start(bf16[128,768]{1,0:T(8,128)(2,1)S(1)} %constant_dynamic-update-slice_fusion.2.refs_0_), channel_id=1, source_target_pairs={{0,16},{4,20},{8,24},{12,28},{16,0},{20,4},{24,8},{28,12},{1,17},{... | collective-permute-start | bytes 589832 | tf_op jit(solution)/shard_map/ppermute | solution.py:171
  14.0 1.5 %collective-permute-start.2 = (bf16[128,768]{1,0:T(8,128)(2,1)S(1)}, bf16[128,768]{1,0:T(8,128)(2,1)S(1)}, u32[]{:S(2)}, u32[]{:S(2)}) collective-permute-start(bf16[128,768]{1,0:T(8,128)(2,1)S(1)} %constant_dynamic-update-slice_fusion.2.refs_0_), channel_id=1, source_target_pairs={{0,8},{4,12},{8,0},{12,4},{16,24},{20,28},{24,16},{28,20},{1,9},{5... | collective-permute-start | bytes 589832 | tf_op jit(solution)/shard_map/ppermute | solution.py:171
  15.5 0.0 collective-permute-done.4.refs_3_
  15.5 1.2 %collective-permute-start.5 = (bf16[64,768]{1,0:T(8,128)(2,1)S(1)}, bf16[64,768]{1,0:T(8,128)(2,1)S(1)}, u32[]{:S(2)}, u32[]{:S(2)}) collective-permute-start(bf16[64,768]{1,0:T(8,128)(2,1)S(1)} %collective-permute-done.4.refs_3_), channel_id=1, source_target_pairs={{0,1},{1,0},{2,3},{3,2},{4,5},{5,4},{6,7},{7,6},{8,9},{9,8},{10,11... | collective-permute-start | bytes 294920 | tf_op jit(solution)/shard_map/ppermute | solution.py:171
  16.7 0.0 copy-done.1
  16.7 0.0 copy-start
  16.7 1.1 %copy-done = bf16[512,768]{1,0:T(8,128)(2,1)S(1)} copy-done((bf16[512,768]{1,0:T(8,128)(2,1)S(1)}, bf16[512,768]{1,0:T(8,128)(2,1)}, u32[]{:S(2)}) %copy-start) | copy-done | bytes 786456
  17.8 0.2 shard_map.50
  18.1 2.1 %collective-permute-done.5.refs_4_ = bf16[64,768]{1,0:T(8,128)(2,1)S(1)} collective-permute-done((bf16[64,768]{1,0:T(8,128)(2,1)S(1)}, bf16[64,768]{1,0:T(8,128)(2,1)S(1)}, u32[]{:S(2)}, u32[]{:S(2)}) %collective-permute-start.5) | collective-permute-done | bytes 98336 | tf_op jit(solution)/shard_map/ppermute | solution.py:171
  20.2 0.0 collective-permute-done.3.refs_2_
  20.2 0.0 collective-permute-done.2.refs_1_
  20.2 0.0 collective-permute-start.6
  20.2 0.5 %collective-permute-start.7 = (bf16[128,768]{1,0:T(8,128)(2,1)S(1)}, bf16[128,768]{1,0:T(8,128)(2,1)S(1)}, u32[]{:S(2)}, u32[]{:S(2)}) collective-permute-start(bf16[128,768]{1,0:T(8,128)(2,1)S(1)} %collective-permute-done.2.refs_1_), channel_id=1, source_target_pairs={{0,4},{4,0},{8,12},{12,8},{16,20},{20,16},{24,28},{28,24},{1,5},{5... | collective-permute-start | bytes 589832 | tf_op jit(solution)/shard_map/ppermute | solution.py:171
  20.7 0.1 collective-permute-start.8
  20.8 0.4 %collective-permute-start.9 = (bf16[64,768]{1,0:T(8,128)(2,1)S(1)}, bf16[64,768]{1,0:T(8,128)(2,1)S(1)}, u32[]{:S(2)}, u32[]{:S(2)}) collective-permute-start(bf16[64,768]{1,0:T(8,128)(2,1)S(1)} %collective-permute-done.4.refs_3_), channel_id=1, source_target_pairs={{0,4},{4,0},{8,12},{12,8},{16,20},{20,16},{24,28},{28,24},{1,5},{5... | collective-permute-start | bytes 294920 | tf_op jit(solution)/shard_map/ppermute | solution.py:171
  21.2 0.1 collective-permute-start.10
  21.3 1.0 %shard_map.51 = (bf16[512,768]{1,0:T(8,128)(2,1)S(1)}, f32[1,512]{1,0:T(1,128)S(1)}, f32[512,512]{1,0:T(8,128)S(1)}, f32[512,1]{1,0:T(8,128)S(1)}, f32[512,1]{1,0:T(8,128)S(1)}, /*index=5*/f32[512,1]{1,0:T(8,128)S(1)}) custom-call(s32[512,1]{1,0:T(8,128)S(1)} %get-tuple-element.27.spot_ref, bf16[512,768]{1,0:T(8,128)(2,1)S(1)} %get-tuple-element.28.q_ref, ...), custom_call_target="tpu_custom_call" | custom-call | flops 512 | bytes 512 | tf_op jit(solution)/shard_map/pallas_call | solution.py:201
  22.3 0.1 collective-permute-done.9.refs_9_
  22.3 0.2 collective-permute-done.10.refs_10_
  22.5 0.0 collective-permute-done.6.refs_6_
  22.5 0.0 collective-permute-done.7.refs_7_
  22.5 0.0 collective-permute-done.8.refs_8_
  22.5 2.8 %shard_map.52 = (f32[1,512]{1,0:T(1,128)}, bf16[512,768]{1,0:T(8,128)(2,1)}) custom-call(s32[512,1]{1,0:T(8,128)S(1)} %get-tuple-element.27.spot_ref, bf16[512,768]{1,0:T(8,128)(2,1)S(1)} %get-tuple-element.28.q_ref, bf16[512,768]{1,0:T(8,128)(2,1)S(1)} %get-tuple-element.34.refs_0_, f32[1,512]{1,0:T(1,128)S(1)} %get-tuple-element.35.refs_1_, ...), custom_call_target="tpu_custom_call" | custom-call | flops 512 | bytes 512 | tf_op jit(solution)/shard_map/pallas_call | solution.py:237
  (2 shorter events, 0.0 us)
Async XLA Ops:
  0.6 6.9 %collective-permute-start = (bf16[32,768]{1,0:T(8,128)(2,1)}, bf16[32,768]{1,0:T(8,128)(2,1)S(1)}, u32[]{:S(2)}, u32[]{:S(2)}) collective-permute-start(bf16[32,768]{1,0:T(8,128)(2,1)} %param.4), channel_id=1, source_target_pairs={{0,2},{1,3},{2,0},{3,1},{4,6},{5,7},{6,4},{7,5},{8,10},{9,11},{10,... | collective-permute-start | bytes 147464 | tf_op jit(solution)/shard_map/ppermute | solution.py:171
  7.5 4.7 %collective-permute-start.1 = (bf16[64,768]{1,0:T(8,128)(2,1)S(1)}, bf16[64,768]{1,0:T(8,128)(2,1)S(1)}, u32[]{:S(2)}, u32[]{:S(2)}) collective-permute-start(bf16[64,768]{1,0:T(8,128)(2,1)S(1)} %get-tuple-element.42), channel_id=1, source_target_pairs={{0,1},{1,0},{2,3},{3,2},{4,5},{5,4},{6,7},{7,6},{8,9},{9,8},{10,11... | collective-permute-start | bytes 294920 | tf_op jit(solution)/shard_map/ppermute | solution.py:171
  9.0 6.6 %collective-permute-start.4 = (bf16[64,768]{1,0:T(8,128)(2,1)S(1)}, bf16[64,768]{1,0:T(8,128)(2,1)S(1)}, u32[]{:S(2)}, u32[]{:S(2)}) collective-permute-start(bf16[64,768]{1,0:T(8,128)(2,1)S(1)} %get-tuple-element.42), channel_id=1, source_target_pairs={{0,24},{4,28},{8,16},{12,20},{16,8},{20,12},{24,0},{28,4},{1,25},{... | collective-permute-start | bytes 294920 | tf_op jit(solution)/shard_map/ppermute | solution.py:171
  12.2 4.5 %copy-start.1 = (s32[512]{0:T(512)S(1)}, s32[512]{0:T(512)}, u32[]{:S(2)}) copy-start(s32[512]{0:T(512)} %param.5) | copy-start | bytes 6148
  12.2 7.9 %collective-permute-start.3 = (bf16[128,768]{1,0:T(8,128)(2,1)S(1)}, bf16[128,768]{1,0:T(8,128)(2,1)S(1)}, u32[]{:S(2)}, u32[]{:S(2)}) collective-permute-start(bf16[128,768]{1,0:T(8,128)(2,1)S(1)} %constant_dynamic-update-slice_fusion.2.refs_0_), channel_id=1, source_target_pairs={{0,16},{4,20},{8,24},{12,28},{16,0},{20,4},{24,8},{28,12},{1,17},{... | collective-permute-start | bytes 589832 | tf_op jit(solution)/shard_map/ppermute | solution.py:171
  14.0 6.1 %collective-permute-start.2 = (bf16[128,768]{1,0:T(8,128)(2,1)S(1)}, bf16[128,768]{1,0:T(8,128)(2,1)S(1)}, u32[]{:S(2)}, u32[]{:S(2)}) collective-permute-start(bf16[128,768]{1,0:T(8,128)(2,1)S(1)} %constant_dynamic-update-slice_fusion.2.refs_0_), channel_id=1, source_target_pairs={{0,8},{4,12},{8,0},{12,4},{16,24},{20,28},{24,16},{28,20},{1,9},{5... | collective-permute-start | bytes 589832 | tf_op jit(solution)/shard_map/ppermute | solution.py:171
  15.5 4.6 %collective-permute-start.5 = (bf16[64,768]{1,0:T(8,128)(2,1)S(1)}, bf16[64,768]{1,0:T(8,128)(2,1)S(1)}, u32[]{:S(2)}, u32[]{:S(2)}) collective-permute-start(bf16[64,768]{1,0:T(8,128)(2,1)S(1)} %collective-permute-done.4.refs_3_), channel_id=1, source_target_pairs={{0,1},{1,0},{2,3},{3,2},{4,5},{5,4},{6,7},{7,6},{8,9},{9,8},{10,11... | collective-permute-start | bytes 294920 | tf_op jit(solution)/shard_map/ppermute | solution.py:171
  16.7 1.1 %copy-start = (bf16[512,768]{1,0:T(8,128)(2,1)S(1)}, bf16[512,768]{1,0:T(8,128)(2,1)}, u32[]{:S(2)}) copy-start(bf16[512,768]{1,0:T(8,128)(2,1)} %queries_hbm) | copy-start | bytes 2359300
  20.2 2.3 %collective-permute-start.6 = (bf16[128,768]{1,0:T(8,128)(2,1)S(1)}, bf16[128,768]{1,0:T(8,128)(2,1)S(1)}, u32[]{:S(2)}, u32[]{:S(2)}) collective-permute-start(bf16[128,768]{1,0:T(8,128)(2,1)S(1)} %constant_dynamic-update-slice_fusion.2.refs_0_), channel_id=1, source_target_pairs={{0,4},{4,0},{8,12},{12,8},{16,20},{20,16},{24,28},{28,24},{1,5},{5... | collective-permute-start | bytes 589832 | tf_op jit(solution)/shard_map/ppermute | solution.py:171
  20.2 2.3 %collective-permute-start.7 = (bf16[128,768]{1,0:T(8,128)(2,1)S(1)}, bf16[128,768]{1,0:T(8,128)(2,1)S(1)}, u32[]{:S(2)}, u32[]{:S(2)}) collective-permute-start(bf16[128,768]{1,0:T(8,128)(2,1)S(1)} %collective-permute-done.2.refs_1_), channel_id=1, source_target_pairs={{0,4},{4,0},{8,12},{12,8},{16,20},{20,16},{24,28},{28,24},{1,5},{5... | collective-permute-start | bytes 589832 | tf_op jit(solution)/shard_map/ppermute | solution.py:171
  20.7 1.8 %collective-permute-start.8 = (bf16[128,768]{1,0:T(8,128)(2,1)S(1)}, bf16[128,768]{1,0:T(8,128)(2,1)S(1)}, u32[]{:S(2)}, u32[]{:S(2)}) collective-permute-start(bf16[128,768]{1,0:T(8,128)(2,1)S(1)} %collective-permute-done.3.refs_2_), channel_id=1, source_target_pairs={{0,4},{4,0},{8,12},{12,8},{16,20},{20,16},{24,28},{28,24},{1,5},{5... | collective-permute-start | bytes 589832 | tf_op jit(solution)/shard_map/ppermute | solution.py:171
  20.8 1.6 %collective-permute-start.9 = (bf16[64,768]{1,0:T(8,128)(2,1)S(1)}, bf16[64,768]{1,0:T(8,128)(2,1)S(1)}, u32[]{:S(2)}, u32[]{:S(2)}) collective-permute-start(bf16[64,768]{1,0:T(8,128)(2,1)S(1)} %collective-permute-done.4.refs_3_), channel_id=1, source_target_pairs={{0,4},{4,0},{8,12},{12,8},{16,20},{20,16},{24,28},{28,24},{1,5},{5... | collective-permute-start | bytes 294920 | tf_op jit(solution)/shard_map/ppermute | solution.py:171
  21.2 1.3 %collective-permute-start.10 = (bf16[64,768]{1,0:T(8,128)(2,1)S(1)}, bf16[64,768]{1,0:T(8,128)(2,1)S(1)}, u32[]{:S(2)}, u32[]{:S(2)}) collective-permute-start(bf16[64,768]{1,0:T(8,128)(2,1)S(1)} %collective-permute-done.5.refs_4_), channel_id=1, source_target_pairs={{0,4},{4,0},{8,12},{12,8},{16,20},{20,16},{24,28},{28,24},{1,5},{5... | collective-permute-start | bytes 294920 | tf_op jit(solution)/shard_map/ppermute | solution.py:171

commit v4 on v3

--- a/solution.py
+++ b/solution.py
@@ -164,7 +164,8 @@
     block = min(rows, 256)
     far = range(2, wide, 2)
     evens = list(range(0, narrow, 2))
-    order = evens + [k ^ 1 for k in evens]
+    bent_order = evens + [k ^ 1 for k in evens]
+    straight_order = [k ^ (k >> 1) for k in range(narrow)]
 
     def swap(array, axis, bits):
         size = wide if axis == "wide" else narrow
@@ -193,7 +194,12 @@
         )(positives.reshape(1, rows), queries)
 
     def bases_of(distances):
-        return [(k * narrow + n) * own for k in distances for n in order]
+        bases = []
+        for k in distances:
+            far_k = k - k % 2
+            order = bent_order if far_k & (far_k - 1) else straight_order
+            bases += [(k * narrow + n) * own for n in order]
+        return bases
 
     def score(spots, loaded, distances, chunks):
         docs = len(distances) * own * narrow
@@ -213,11 +219,10 @@
             **params(docs, docs),
         )(spots, loaded, *chunks)
 
-    shard = {0: documents} | {k: swap(documents, "narrow", k) for k in evens[1:]}
+    shard = {0: documents} | {k: swap(documents, "narrow", k) for k in straight_order[1:]}
     base = jnp.concatenate([shard[k] for k in evens], axis=0)
     firsts = {k: swap(base, "wide", k) for k in far if k & (k - 1)}
-    other = swap(base, "narrow", 1)
-    column = jnp.concatenate([base, other], axis=0)
+    column = jnp.concatenate([shard[k] for k in straight_order], axis=0)
     held = {}
     for k in far:
         if k & (k - 1) == 0:

time: 25.5 us -> 24.8 us (0.973)
  waiting for transfers between devices: 5.11 us -> 2.49 us
  starting transfers between devices: 13.5 us -> 15.3 us
    ppermute x11 -> x12, waiting for transfers between devices: 5.11 us -> 2.49 us  [swap(): return lax.ppermute(array, axis, [(i, i ^ bits) for i in range(size)])]
    ppermute x11 -> x12, starting transfers between devices: 13.5 us -> 15.3 us  [swap(): return lax.ppermute(array, axis, [(i, i ^ bits) for i in range(size)])]
    unnamed x5 -> x9, local copies, waits for them, and re-layouts: 1.98 us -> 1.98 us
  transfers between devices with their start and end apart: 11 -> 12, of which waited for: 5 -> 6; matrix products, arithmetic and copies ran while one was open for 3% -> 3% of each run, Pallas kernels for 5% -> 5%
where the time goes in v4:
time: 24.8 us; the launch traced here: 24.5 us
  starting transfers between devices  15.3 us (62%)
  Pallas kernels  4.05 us (16%)
  waiting for transfers between devices  2.49 us (10%)
  local copies, waits for them, and re-layouts  1.99 us (8%)
  between operations  0.68 us (3%)
    ppermute x12, starting transfers between devices, swap(): return lax.ppermute(array, axis, [(i, i ^ bits) for i in range(size)])  15.3 us
    pallas_call x1, Pallas kernels, shards(): pl.pallas_call(functools.partial(late_kernel, bases, own, block), out_sha...  2.83 us
    ppermute x12, waiting for transfers between devices, swap(): return lax.ppermute(array, axis, [(i, i ^ bits) for i in range(size)])  2.49 us
    unnamed x9, local copies, waits for them, and re-layouts  1.98 us
    pallas_call x1, Pallas kernels, score(): pl.pallas_call(functools.partial(early_kernel, bases_of(distances), own,...  0.99 us
  transfers between devices with their start and end apart: 12, of which 6 were waited for; matrix products, arithmetic and copies ran while one was open for 3% of the time, Pallas kernels for 5%

profile of v4, /device:TPU:0, one launch (start us, length us, event | category | flops | bytes accessed | tf_op | source)
XLA Modules:
  0.0 24.5 jit_solution(9700889649130944706)
XLA Ops:
  0.6 0.0 copy-start.2
  0.6 4.1 %collective-permute-start.2 = (bf16[32,768]{1,0:T(8,128)(2,1)}, bf16[32,768]{1,0:T(8,128)(2,1)S(1)}, u32[]{:S(2)}, u32[]{:S(2)}) collective-permute-start(bf16[32,768]{1,0:T(8,128)(2,1)} %param.4), channel_id=1, source_target_pairs={{0,2},{1,3},{2,0},{3,1},{4,6},{5,7},{6,4},{7,5},{8,10},{9,11},{10,... | collective-permute-start | bytes 147464 | tf_op jit(solution)/shard_map/ppermute | solution.py:172
  4.7 1.3 %collective-permute-start.1 = (bf16[32,768]{1,0:T(8,128)(2,1)}, bf16[32,768]{1,0:T(8,128)(2,1)S(1)}, u32[]{:S(2)}, u32[]{:S(2)}) collective-permute-start(bf16[32,768]{1,0:T(8,128)(2,1)} %param.4), channel_id=1, source_target_pairs={{0,3},{1,2},{2,1},{3,0},{4,7},{5,6},{6,5},{7,4},{8,11},{9,10},{10,... | collective-permute-start | bytes 147464 | tf_op jit(solution)/shard_map/ppermute | solution.py:172
  6.1 0.2 collective-permute-start
  6.3 0.8 %constant_dynamic-update-slice_fusion.3 = bf16[128,768]{1,0:T(8,128)(2,1)S(1)} fusion(bf16[32,768]{1,0:T(8,128)(2,1)} %param.4), kind=kLoop, calls=%fused_computation.4 | loop fusion | bytes 98304
  7.2 0.4 %collective-permute-done.2 = bf16[32,768]{1,0:T(8,128)(2,1)S(1)} collective-permute-done((bf16[32,768]{1,0:T(8,128)(2,1)}, bf16[32,768]{1,0:T(8,128)(2,1)S(1)}, u32[]{:S(2)}, u32[]{:S(2)}) %collective-permute-start.2) | collective-permute-done | bytes 49184 | tf_op jit(solution)/shard_map/ppermute | solution.py:172
  7.5 0.0 copy-done.2
  7.6 2.7 %collective-permute-start.5 = (bf16[64,768]{1,0:T(8,128)(2,1)S(1)}, bf16[64,768]{1,0:T(8,128)(2,1)S(1)}, u32[]{:S(2)}, u32[]{:S(2)}) collective-permute-start(bf16[64,768]{1,0:T(8,128)(2,1)S(1)} %pad_maximum_fusion), channel_id=1, source_target_pairs={{0,24},{4,28},{8,16},{12,20},{16,8},{20,12},{24,0},{28,4},{1,25},{... | collective-permute-start | bytes 294920 | tf_op jit(solution)/shard_map/ppermute | solution.py:172
  10.3 0.1 collective-permute-done
  10.4 0.5 %collective-permute-done.1 = bf16[32,768]{1,0:T(8,128)(2,1)S(1)} collective-permute-done((bf16[32,768]{1,0:T(8,128)(2,1)}, bf16[32,768]{1,0:T(8,128)(2,1)S(1)}, u32[]{:S(2)}, u32[]{:S(2)}) %collective-permute-start.1) | collective-permute-done | bytes 49184 | tf_op jit(solution)/shard_map/ppermute | solution.py:172
  10.9 0.0 copy-start.1
  10.9 1.6 %collective-permute-start.4 = (bf16[128,768]{1,0:T(8,128)(2,1)S(1)}, bf16[128,768]{1,0:T(8,128)(2,1)S(1)}, u32[]{:S(2)}, u32[]{:S(2)}) collective-permute-start(bf16[128,768]{1,0:T(8,128)(2,1)S(1)} %constant_dynamic-update-slice_fusion.refs_0_), channel_id=1, source_target_pairs={{0,16},{4,20},{8,24},{12,28},{16,0},{20,4},{24,8},{28,12},{1,17},{... | collective-permute-start | bytes 589832 | tf_op jit(solution)/shard_map/ppermute | solution.py:172
  12.5 1.5 %collective-permute-start.3 = (bf16[128,768]{1,0:T(8,128)(2,1)S(1)}, bf16[128,768]{1,0:T(8,128)(2,1)S(1)}, u32[]{:S(2)}, u32[]{:S(2)}) collective-permute-start(bf16[128,768]{1,0:T(8,128)(2,1)S(1)} %constant_dynamic-update-slice_fusion.refs_0_), channel_id=1, source_target_pairs={{0,8},{4,12},{8,0},{12,4},{16,24},{20,28},{24,16},{28,20},{1,9},{5... | collective-permute-start | bytes 589832 | tf_op jit(solution)/shard_map/ppermute | solution.py:172
  14.0 0.0 collective-permute-done.5.refs_3_
  14.0 2.7 %collective-permute-start.6 = (bf16[64,768]{1,0:T(8,128)(2,1)S(1)}, bf16[64,768]{1,0:T(8,128)(2,1)S(1)}, u32[]{:S(2)}, u32[]{:S(2)}) collective-permute-start(bf16[64,768]{1,0:T(8,128)(2,1)S(1)} %collective-permute-done.5.refs_3_), channel_id=1, source_target_pairs={{0,1},{1,0},{2,3},{3,2},{4,5},{5,4},{6,7},{7,6},{8,9},{9,8},{10,11... | collective-permute-start | bytes 294920 | tf_op jit(solution)/shard_map/ppermute | solution.py:172
  16.8 0.0 copy-done.1
  16.8 0.0 copy-start
  16.8 1.1 %copy-done = bf16[512,768]{1,0:T(8,128)(2,1)S(1)} copy-done((bf16[512,768]{1,0:T(8,128)(2,1)S(1)}, bf16[512,768]{1,0:T(8,128)(2,1)}, u32[]{:S(2)}) %copy-start) | copy-done | bytes 786456
  17.9 0.2 shard_map.50
  18.1 1.2 %collective-permute-done.6.refs_4_ = bf16[64,768]{1,0:T(8,128)(2,1)S(1)} collective-permute-done((bf16[64,768]{1,0:T(8,128)(2,1)S(1)}, bf16[64,768]{1,0:T(8,128)(2,1)S(1)}, u32[]{:S(2)}, u32[]{:S(2)}) %collective-permute-start.6) | collective-permute-done | bytes 98336 | tf_op jit(solution)/shard_map/ppermute | solution.py:172
  19.4 0.0 collective-permute-done.4.refs_2_
  19.4 0.0 collective-permute-done.3.refs_1_
  19.4 0.0 collective-permute-start.7
  19.4 0.5 %collective-permute-start.8 = (bf16[128,768]{1,0:T(8,128)(2,1)S(1)}, bf16[128,768]{1,0:T(8,128)(2,1)S(1)}, u32[]{:S(2)}, u32[]{:S(2)}) collective-permute-start(bf16[128,768]{1,0:T(8,128)(2,1)S(1)} %collective-permute-done.3.refs_1_), channel_id=1, source_target_pairs={{0,4},{4,0},{8,12},{12,8},{16,20},{20,16},{24,28},{28,24},{1,5},{5... | collective-permute-start | bytes 589832 | tf_op jit(solution)/shard_map/ppermute | solution.py:172
  19.9 0.1 collective-permute-start.9
  19.9 0.4 %collective-permute-start.10 = (bf16[64,768]{1,0:T(8,128)(2,1)S(1)}, bf16[64,768]{1,0:T(8,128)(2,1)S(1)}, u32[]{:S(2)}, u32[]{:S(2)}) collective-permute-start(bf16[64,768]{1,0:T(8,128)(2,1)S(1)} %collective-permute-done.5.refs_3_), channel_id=1, source_target_pairs={{0,4},{4,0},{8,12},{12,8},{16,20},{20,16},{24,28},{28,24},{1,5},{5... | collective-permute-start | bytes 294920 | tf_op jit(solution)/shard_map/ppermute | solution.py:172
  20.4 0.1 collective-permute-start.11
  20.5 1.0 %shard_map.51 = (bf16[512,768]{1,0:T(8,128)(2,1)S(1)}, f32[1,512]{1,0:T(1,128)S(1)}, f32[512,512]{1,0:T(8,128)S(1)}, f32[512,1]{1,0:T(8,128)S(1)}, f32[512,1]{1,0:T(8,128)S(1)}, /*index=5*/f32[512,1]{1,0:T(8,128)S(1)}) custom-call(s32[512,1]{1,0:T(8,128)S(1)} %get-tuple-element.27.spot_ref, bf16[512,768]{1,0:T(8,128)(2,1)S(1)} %get-tuple-element.28.q_ref, ...), custom_call_target="tpu_custom_call" | custom-call | flops 512 | bytes 512 | tf_op jit(solution)/shard_map/pallas_call | solution.py:207
  21.4 0.1 collective-permute-done.10.refs_9_
  21.5 0.2 collective-permute-done.11.refs_10_
  21.7 0.0 collective-permute-done.7.refs_6_
  21.7 0.0 collective-permute-done.8.refs_7_
  21.7 0.0 collective-permute-done.9.refs_8_
  21.7 2.8 %shard_map.52 = (f32[1,512]{1,0:T(1,128)}, bf16[512,768]{1,0:T(8,128)(2,1)}) custom-call(s32[512,1]{1,0:T(8,128)S(1)} %get-tuple-element.27.spot_ref, bf16[512,768]{1,0:T(8,128)(2,1)S(1)} %get-tuple-element.28.q_ref, bf16[512,768]{1,0:T(8,128)(2,1)S(1)} %get-tuple-element.34.refs_0_, f32[1,512]{1,0:T(1,128)S(1)} %get-tuple-element.35.refs_1_, ...), custom_call_target="tpu_custom_call" | custom-call | flops 512 | bytes 512 | tf_op jit(solution)/shard_map/pallas_call | solution.py:242
  (4 shorter events, 0.0 us)
Async XLA Ops:
  0.6 6.9 %copy-start.2 = (bf16[32,768]{1,0:T(8,128)(2,1)S(1)}, bf16[32,768]{1,0:T(8,128)(2,1)}, u32[]{:S(2)}) copy-start(bf16[32,768]{1,0:T(8,128)(2,1)} %param.4) | copy-start | bytes 147460
  0.6 6.9 %collective-permute-start.2 = (bf16[32,768]{1,0:T(8,128)(2,1)}, bf16[32,768]{1,0:T(8,128)(2,1)S(1)}, u32[]{:S(2)}, u32[]{:S(2)}) collective-permute-start(bf16[32,768]{1,0:T(8,128)(2,1)} %param.4), channel_id=1, source_target_pairs={{0,2},{1,3},{2,0},{3,1},{4,6},{5,7},{6,4},{7,5},{8,10},{9,11},{10,... | collective-permute-start | bytes 147464 | tf_op jit(solution)/shard_map/ppermute | solution.py:172
  4.7 6.2 %collective-permute-start.1 = (bf16[32,768]{1,0:T(8,128)(2,1)}, bf16[32,768]{1,0:T(8,128)(2,1)S(1)}, u32[]{:S(2)}, u32[]{:S(2)}) collective-permute-start(bf16[32,768]{1,0:T(8,128)(2,1)} %param.4), channel_id=1, source_target_pairs={{0,3},{1,2},{2,1},{3,0},{4,7},{5,6},{6,5},{7,4},{8,11},{9,10},{10,... | collective-permute-start | bytes 147464 | tf_op jit(solution)/shard_map/ppermute | solution.py:172
  6.1 4.3 %collective-permute-start = (bf16[32,768]{1,0:T(8,128)(2,1)}, bf16[32,768]{1,0:T(8,128)(2,1)S(1)}, u32[]{:S(2)}, u32[]{:S(2)}) collective-permute-start(bf16[32,768]{1,0:T(8,128)(2,1)} %param.4), channel_id=1, source_target_pairs={{0,1},{1,0},{2,3},{3,2},{4,5},{5,4},{6,7},{7,6},{8,9},{9,8},{10,11... | collective-permute-start | bytes 147464 | tf_op jit(solution)/shard_map/ppermute | solution.py:172
  7.6 6.5 %collective-permute-start.5 = (bf16[64,768]{1,0:T(8,128)(2,1)S(1)}, bf16[64,768]{1,0:T(8,128)(2,1)S(1)}, u32[]{:S(2)}, u32[]{:S(2)}) collective-permute-start(bf16[64,768]{1,0:T(8,128)(2,1)S(1)} %pad_maximum_fusion), channel_id=1, source_target_pairs={{0,24},{4,28},{8,16},{12,20},{16,8},{20,12},{24,0},{28,4},{1,25},{... | collective-permute-start | bytes 294920 | tf_op jit(solution)/shard_map/ppermute | solution.py:172
  10.9 5.8 %copy-start.1 = (s32[512]{0:T(512)S(1)}, s32[512]{0:T(512)}, u32[]{:S(2)}) copy-start(s32[512]{0:T(512)} %param.5) | copy-start | bytes 6148
  10.9 8.4 %collective-permute-start.4 = (bf16[128,768]{1,0:T(8,128)(2,1)S(1)}, bf16[128,768]{1,0:T(8,128)(2,1)S(1)}, u32[]{:S(2)}, u32[]{:S(2)}) collective-permute-start(bf16[128,768]{1,0:T(8,128)(2,1)S(1)} %constant_dynamic-update-slice_fusion.refs_0_), channel_id=1, source_target_pairs={{0,16},{4,20},{8,24},{12,28},{16,0},{20,4},{24,8},{28,12},{1,17},{... | collective-permute-start | bytes 589832 | tf_op jit(solution)/shard_map/ppermute | solution.py:172
  12.5 6.8 %collective-permute-start.3 = (bf16[128,768]{1,0:T(8,128)(2,1)S(1)}, bf16[128,768]{1,0:T(8,128)(2,1)S(1)}, u32[]{:S(2)}, u32[]{:S(2)}) collective-permute-start(bf16[128,768]{1,0:T(8,128)(2,1)S(1)} %constant_dynamic-update-slice_fusion.refs_0_), channel_id=1, source_target_pairs={{0,8},{4,12},{8,0},{12,4},{16,24},{20,28},{24,16},{28,20},{1,9},{5... | collective-permute-start | bytes 589832 | tf_op jit(solution)/shard_map/ppermute | solution.py:172
  14.0 5.3 %collective-permute-start.6 = (bf16[64,768]{1,0:T(8,128)(2,1)S(1)}, bf16[64,768]{1,0:T(8,128)(2,1)S(1)}, u32[]{:S(2)}, u32[]{:S(2)}) collective-permute-start(bf16[64,768]{1,0:T(8,128)(2,1)S(1)} %collective-permute-done.5.refs_3_), channel_id=1, source_target_pairs={{0,1},{1,0},{2,3},{3,2},{4,5},{5,4},{6,7},{7,6},{8,9},{9,8},{10,11... | collective-permute-start | bytes 294920 | tf_op jit(solution)/shard_map/ppermute | solution.py:172
  16.8 1.1 %copy-start = (bf16[512,768]{1,0:T(8,128)(2,1)S(1)}, bf16[512,768]{1,0:T(8,128)(2,1)}, u32[]{:S(2)}) copy-start(bf16[512,768]{1,0:T(8,128)(2,1)} %queries_hbm) | copy-start | bytes 2359300
  19.4 2.3 %collective-permute-start.7 = (bf16[128,768]{1,0:T(8,128)(2,1)S(1)}, bf16[128,768]{1,0:T(8,128)(2,1)S(1)}, u32[]{:S(2)}, u32[]{:S(2)}) collective-permute-start(bf16[128,768]{1,0:T(8,128)(2,1)S(1)} %constant_dynamic-update-slice_fusion.refs_0_), channel_id=1, source_target_pairs={{0,4},{4,0},{8,12},{12,8},{16,20},{20,16},{24,28},{28,24},{1,5},{5... | collective-permute-start | bytes 589832 | tf_op jit(solution)/shard_map/ppermute | solution.py:172
  19.4 2.3 %collective-permute-start.8 = (bf16[128,768]{1,0:T(8,128)(2,1)S(1)}, bf16[128,768]{1,0:T(8,128)(2,1)S(1)}, u32[]{:S(2)}, u32[]{:S(2)}) collective-permute-start(bf16[128,768]{1,0:T(8,128)(2,1)S(1)} %collective-permute-done.3.refs_1_), channel_id=1, source_target_pairs={{0,4},{4,0},{8,12},{12,8},{16,20},{20,16},{24,28},{28,24},{1,5},{5... | collective-permute-start | bytes 589832 | tf_op jit(solution)/shard_map/ppermute | solution.py:172
  19.9 1.8 %collective-permute-start.9 = (bf16[128,768]{1,0:T(8,128)(2,1)S(1)}, bf16[128,768]{1,0:T(8,128)(2,1)S(1)}, u32[]{:S(2)}, u32[]{:S(2)}) collective-permute-start(bf16[128,768]{1,0:T(8,128)(2,1)S(1)} %collective-permute-done.4.refs_2_), channel_id=1, source_target_pairs={{0,4},{4,0},{8,12},{12,8},{16,20},{20,16},{24,28},{28,24},{1,5},{5... | collective-permute-start | bytes 589832 | tf_op jit(solution)/shard_map/ppermute | solution.py:172
  19.9 1.6 %collective-permute-start.10 = (bf16[64,768]{1,0:T(8,128)(2,1)S(1)}, bf16[64,768]{1,0:T(8,128)(2,1)S(1)}, u32[]{:S(2)}, u32[]{:S(2)}) collective-permute-start(bf16[64,768]{1,0:T(8,128)(2,1)S(1)} %collective-permute-done.5.refs_3_), channel_id=1, source_target_pairs={{0,4},{4,0},{8,12},{12,8},{16,20},{20,16},{24,28},{28,24},{1,5},{5... | collective-permute-start | bytes 294920 | tf_op jit(solution)/shard_map/ppermute | solution.py:172
  20.4 1.3 %collective-permute-start.11 = (bf16[64,768]{1,0:T(8,128)(2,1)S(1)}, bf16[64,768]{1,0:T(8,128)(2,1)S(1)}, u32[]{:S(2)}, u32[]{:S(2)}) collective-permute-start(bf16[64,768]{1,0:T(8,128)(2,1)S(1)} %collective-permute-done.6.refs_4_), channel_id=1, source_target_pairs={{0,4},{4,0},{8,12},{12,8},{16,20},{20,16},{24,28},{28,24},{1,5},{5... | collective-permute-start | bytes 294920 | tf_op jit(solution)/shard_map/ppermute | solution.py:172

commit v5 on v2

--- a/solution.py
+++ b/solution.py
@@ -63,11 +63,16 @@
     return lax.dot_general(q, codes, NT, preferred_element_type=jnp.float32)
 
 
-def load_kernel(narrow, own, positives_hbm, queries_hbm, spot_ref, q_ref, positives_ref, sem):
+def load_kernel(narrow, own, positives_hbm, queries_hbm, *refs):
+    parts, (spot_ref, q_ref, packed_ref, positives_ref, sem) = refs[:-5], refs[-5:]
     fetch = pltpu.make_async_copy(positives_hbm, positives_ref, sem.at[0])
     fetch.start()
     copy = pltpu.make_async_copy(queries_hbm, q_ref, sem.at[1])
     copy.start()
+    start = 0
+    for part in parts:
+        packed_ref[pl.ds(start, part.shape[0]), :] = part[...]
+        start += part.shape[0]
     fetch.wait()
     me = lax.axis_index("wide") * narrow + lax.axis_index("narrow")
     local = (positives_ref[...] ^ (me * own)).astype(jnp.float32)
@@ -163,10 +168,17 @@
     barrier = lax.optimization_barrier
     block = min(rows, 256)
     far = range(2, wide, 2)
-
-    def swap(array, axis, bits):
-        size = wide if axis == "wide" else narrow
-        return lax.ppermute(array, axis, [(i, i ^ bits) for i in range(size)])
+    evens = list(range(0, narrow, 2))
+    straight_order = [k ^ (k >> 1) for k in range(narrow)]
+
+    def swap(chunk, bits, step=0):
+        array, places = chunk
+        jump = bits * narrow + step
+        pairs = [(i, i ^ jump) for i in range(wide * narrow)]
+        return lax.ppermute(array, AXES, pairs), [place ^ jump for place in places]
+
+    def join(chunks):
+        return jnp.concatenate([c[0] for c in chunks], axis=0), [p for c in chunks for p in c[1]]
 
     def params(docs, kept):
         held = 6 * docs * width + 8 * rows * width + 4 * rows * (kept + 512) + 12 * block * docs
@@ -177,27 +189,29 @@
             cost_estimate=pl.CostEstimate(flops=rows, bytes_accessed=rows, transcendentals=0),
         )
 
-    def load(positives, queries):
+    def load(positives, queries, parts):
         return pl.pallas_call(
             functools.partial(load_kernel, narrow, own),
             out_shape=(
                 jax.ShapeDtypeStruct((rows, 1), jnp.int32),
                 jax.ShapeDtypeStruct((rows, width), bf16),
+                jax.ShapeDtypeStruct((sum(part.shape[0] for part in parts), width), bf16),
             ),
-            in_specs=[HBM, HBM],
-            out_specs=(VMEM, VMEM),
+            in_specs=[HBM, HBM] + [VMEM] * len(parts),
+            out_specs=(VMEM, VMEM, VMEM),
             scratch_shapes=[pltpu.VMEM((1, rows), jnp.int32), pltpu.SemaphoreType.DMA((2,))],
-            **params(0, 0),
-        )(positives.reshape(1, rows), queries)
-
-    def bases_of(distances):
-        return [(k * narrow + n) * own for k in distances for n in range(narrow)]
-
-    def score(spots, loaded, distances, chunks):
-        docs = len(chunks) * own * narrow
+            **params(own * narrow * wide // 2, 0),
+        )(positives.reshape(1, rows), queries, *parts)
+
+    def bases_of(chunks):
+        return [place * own for _, places in chunks for place in places]
+
+    def score(spots, loaded, chunks):
+        bases = bases_of(chunks)
+        docs = len(bases) * own
         column = jax.ShapeDtypeStruct((rows, 1), f32)
         return pl.pallas_call(
-            functools.partial(early_kernel, bases_of(distances), own, block),
+            functools.partial(early_kernel, bases, own, block),
             out_shape=(
                 jax.ShapeDtypeStruct((docs, width), bf16),
                 jax.ShapeDtypeStruct((1, docs), f32),
@@ -209,20 +223,25 @@
             in_specs=[VMEM] * (2 + len(chunks)),
             out_specs=(VMEM,) * 6,
             **params(docs, docs),
-        )(spots, loaded, *chunks)
-
-    shard = {k: swap(documents, "narrow", k) for k in reversed(range(1, narrow))}
-    column = jnp.concatenate([documents] + [shard[k] for k in range(1, narrow)], axis=0)
-    held = {k: swap(column, "wide", k) for k in reversed(far)}
-    column, positives, queries = barrier((column, positives, queries))
-    spots, loaded = load(positives, queries)
-    held[0] = column
-    spots, loaded, held = barrier((spots, loaded, held))
-    mine = range(0, wide, 2)
-    middle = score(spots, loaded, mine, [held[k] for k in mine])
-    mirrored = [swap(held[k], "wide", 1) for k in mine]
+        )(spots, loaded, *[array for array, _ in chunks])
+
+    shard = {0: (documents, [0])}
+    for k in straight_order[1:]:
+        shard[k] = swap(shard[0], 0, k)
+    base = join([shard[k] for k in evens])
+    firsts = [swap(base, k ^ 0) for k in far if k & (k - 1)]
+    column = join([shard[k] for k in straight_order])
+    chunks = [swap(column, k ^ 1) for k in far if k & (k - 1) == 0]
+    chunks += [swap(first, 1, 1) for first in firsts]
+    parts, positives, queries = barrier(([c[0] for c in [column] + firsts], positives, queries))
+    spots, loaded, packed = load(positives, queries, parts)
+    chunks = [(packed, [p for c in [column] + firsts for p in c[1]])] + chunks
+    spots, loaded, arrays = barrier((spots, loaded, [array for array, _ in chunks]))
+    chunks = [(array, places) for array, (_, places) in zip(arrays, chunks)]
+    middle = score(spots, loaded, chunks)
+    mirrored = [swap(chunk, 1) for chunk in chunks]
     docs = own * narrow * wide
-    bases = [bases_of(mine), bases_of([k ^ 1 for k in mine])]
+    bases = [bases_of(chunks), bases_of(mirrored)]
     n_late = len(bases[-1]) * own
     losses, grads = pl.pallas_call(
         functools.partial(late_kernel, bases, own, block),
@@ -242,7 +261,7 @@
             pltpu.SemaphoreType.DMA(()),
         ],
         **params(docs, docs),
-    )(spots, loaded, *middle, *mirrored)
+    )(spots, loaded, *middle, *[array for array, _ in mirrored])
     return losses.reshape(rows), grads
 
 

time: 28 us -> 24 us (0.86)
  waiting for transfers between devices: 10.8 us -> 4.67 us
  starting transfers between devices: 10.2 us -> 12.3 us
    ppermute x10 -> x11, waiting for transfers between devices: 10.8 us -> 4.67 us  [swap(): lax.ppermute(array, AXES, pairs)]
    ppermute x10 -> x11, starting transfers between devices: 10.2 us -> 12.3 us  [swap(): lax.ppermute(array, AXES, pairs)]
    unnamed x7 -> x9, local copies, waits for them, and re-layouts: 2.01 us -> 1.98 us
  transfers between devices with their start and end apart: 10 -> 11, of which waited for: 6 -> 6; matrix products, arithmetic and copies ran while one was open for 3% -> 4% of each run, Pallas kernels for 4% -> 5%
where the time goes in v5:
time: 24 us; the launch traced here: 23.8 us
  starting transfers between devices  12.3 us (51%)
  waiting for transfers between devices  4.67 us (19%)
  Pallas kernels  4.09 us (17%)
  local copies, waits for them, and re-layouts  1.98 us (8%)
  between operations  0.69 us (3%)
    ppermute x11, starting transfers between devices, swap(): lax.ppermute(array, AXES, pairs)  12.3 us
    ppermute x11, waiting for transfers between devices, swap(): lax.ppermute(array, AXES, pairs)  4.67 us
    pallas_call x1, Pallas kernels, shards(): pl.pallas_call(functools.partial(late_kernel, bases, own, block), out_sha...  2.83 us
    unnamed x9, local copies, waits for them, and re-layouts  1.98 us
    pallas_call x1, Pallas kernels, score(): pl.pallas_call(functools.partial(early_kernel, bases, own, block), out_sh...  1.01 us
  transfers between devices with their start and end apart: 11, of which 6 were waited for; matrix products, arithmetic and copies ran while one was open for 4% of the time, Pallas kernels for 5%

profile of v5, /device:TPU:0, one launch (start us, length us, event | category | flops | bytes accessed | tf_op | source)
XLA Modules:
  0.0 23.8 jit_solution(2460448932854110210)
XLA Ops:
  0.6 0.0 copy-start.2
  0.6 4.1 %collective-permute-start.2 = (bf16[32,768]{1,0:T(8,128)(2,1)}, bf16[32,768]{1,0:T(8,128)(2,1)S(1)}, u32[]{:S(2)}, u32[]{:S(2)}) collective-permute-start(bf16[32,768]{1,0:T(8,128)(2,1)} %param.4), channel_id=1, source_target_pairs={{0,2},{1,3},{2,0},{3,1},{4,6},{5,7},{6,4},{7,5},{8,10},{9,11},{10,... | collective-permute-start | bytes 147464 | tf_op jit(solution)/shard_map/ppermute | solution.py:178
  4.7 1.3 %collective-permute-start.1 = (bf16[32,768]{1,0:T(8,128)(2,1)}, bf16[32,768]{1,0:T(8,128)(2,1)S(1)}, u32[]{:S(2)}, u32[]{:S(2)}) collective-permute-start(bf16[32,768]{1,0:T(8,128)(2,1)} %param.4), channel_id=1, source_target_pairs={{0,3},{1,2},{2,1},{3,0},{4,7},{5,6},{6,5},{7,4},{8,11},{9,10},{10,... | collective-permute-start | bytes 147464 | tf_op jit(solution)/shard_map/ppermute | solution.py:178
  6.1 0.2 collective-permute-start
  6.3 0.8 %constant_dynamic-update-slice_fusion.3 = bf16[128,768]{1,0:T(8,128)(2,1)S(1)} fusion(bf16[32,768]{1,0:T(8,128)(2,1)} %param.4), kind=kLoop, calls=%fused_computation.4 | loop fusion | bytes 98304
  7.2 0.4 %collective-permute-done.2 = bf16[32,768]{1,0:T(8,128)(2,1)S(1)} collective-permute-done((bf16[32,768]{1,0:T(8,128)(2,1)}, bf16[32,768]{1,0:T(8,128)(2,1)S(1)}, u32[]{:S(2)}, u32[]{:S(2)}) %collective-permute-start.2) | collective-permute-done | bytes 49184 | tf_op jit(solution)/shard_map/ppermute | solution.py:178
  7.5 0.0 copy-done.2
  7.6 2.7 %collective-permute-start.3 = (bf16[64,768]{1,0:T(8,128)(2,1)S(1)}, bf16[64,768]{1,0:T(8,128)(2,1)S(1)}, u32[]{:S(2)}, u32[]{:S(2)}) collective-permute-start(bf16[64,768]{1,0:T(8,128)(2,1)S(1)} %pad_maximum_fusion), channel_id=1, source_target_pairs={{0,24},{1,25},{2,26},{3,27},{4,28},{5,29},{6,30},{7,31},{8,16},{9,... | collective-permute-start | bytes 294920 | tf_op jit(solution)/shard_map/ppermute | solution.py:178
  10.3 0.1 collective-permute-done
  10.4 0.5 %collective-permute-done.1 = bf16[32,768]{1,0:T(8,128)(2,1)S(1)} collective-permute-done((bf16[32,768]{1,0:T(8,128)(2,1)}, bf16[32,768]{1,0:T(8,128)(2,1)S(1)}, u32[]{:S(2)}, u32[]{:S(2)}) %collective-permute-start.1) | collective-permute-done | bytes 49184 | tf_op jit(solution)/shard_map/ppermute | solution.py:178
  10.9 0.0 copy-start.1
  10.9 0.1 collective-permute-start.5
  11.0 2.7 %collective-permute-start.4 = (bf16[128,768]{1,0:T(8,128)(2,1)S(1)}, bf16[128,768]{1,0:T(8,128)(2,1)S(1)}, u32[]{:S(2)}, u32[]{:S(2)}) collective-permute-start(bf16[128,768]{1,0:T(8,128)(2,1)S(1)} %constant_dynamic-update-slice_fusion.refs_0_), channel_id=1, source_target_pairs={{0,12},{1,13},{2,14},{3,15},{4,8},{5,9},{6,10},{7,11},{8,4},{9,5},... | collective-permute-start | bytes 589832 | tf_op jit(solution)/shard_map/ppermute | solution.py:178
  13.7 0.0 collective-permute-done.3.refs_1_
  13.7 0.0 collective-permute-start.6
  13.7 0.0 copy-done.1
  13.7 0.0 copy-start
  13.8 1.1 %copy-done = bf16[512,768]{1,0:T(8,128)(2,1)S(1)} copy-done((bf16[512,768]{1,0:T(8,128)(2,1)S(1)}, bf16[512,768]{1,0:T(8,128)(2,1)}, u32[]{:S(2)}) %copy-start) | copy-done | bytes 786456
  14.9 0.2 %shard_map.50 = (s32[512,1]{1,0:T(8,128)S(1)}, bf16[512,768]{1,0:T(8,128)(2,1)S(1)}, bf16[192,768]{1,0:T(8,128)(2,1)S(1)}) custom-call(s32[1,512]{1,0:T(1,128)S(1)} %bitcast.2, bf16[512,768]{1,0:T(8,128)(2,1)S(1)} %copy-done, bf16[128,768]{1,0:T(8,128)(2,1)S(1)} %constant_dynamic-update-slice_fusion.refs_0_, bf16[64,768]{1,0:T(8,128)(2,1)S(1)} %collective-permute-done.3.refs_1_), custom_call_target="tpu_custom_call" | custom-call | flops 512 | bytes 512 | tf_op jit(solution)/shard_map/pallas_call | solution.py:193
  15.1 3.0 %collective-permute-done.6.refs_3_ = bf16[64,768]{1,0:T(8,128)(2,1)S(1)} collective-permute-done((bf16[64,768]{1,0:T(8,128)(2,1)S(1)}, bf16[64,768]{1,0:T(8,128)(2,1)S(1)}, u32[]{:S(2)}, u32[]{:S(2)}) %collective-permute-start.6) | collective-permute-done | bytes 98336 | tf_op jit(solution)/shard_map/ppermute | solution.py:178
  18.2 0.0 collective-permute-done.5.refs_2_
  18.2 0.2 collective-permute-done.4.refs_1_
  18.4 0.6 %collective-permute-start.7 = (bf16[192,768]{1,0:T(8,128)(2,1)S(1)}, bf16[192,768]{1,0:T(8,128)(2,1)S(1)}, u32[]{:S(2)}, u32[]{:S(2)}) collective-permute-start(bf16[192,768]{1,0:T(8,128)(2,1)S(1)} %get-tuple-element.32.refs_0_), channel_id=1, source_target_pairs={{0,4},{1,5},{2,6},{3,7},{4,0},{5,1},{6,2},{7,3},{8,12},{9,13},{10,... | collective-permute-start | bytes 884744 | tf_op jit(solution)/shard_map/ppermute | solution.py:178
  19.0 0.0 collective-permute-start.8
  19.0 0.5 %collective-permute-start.9 = (bf16[128,768]{1,0:T(8,128)(2,1)S(1)}, bf16[128,768]{1,0:T(8,128)(2,1)S(1)}, u32[]{:S(2)}, u32[]{:S(2)}) collective-permute-start(bf16[128,768]{1,0:T(8,128)(2,1)S(1)} %collective-permute-done.5.refs_2_), channel_id=1, source_target_pairs={{0,4},{1,5},{2,6},{3,7},{4,0},{5,1},{6,2},{7,3},{8,12},{9,13},{10,... | collective-permute-start | bytes 589832 | tf_op jit(solution)/shard_map/ppermute | solution.py:178
  19.5 0.0 collective-permute-start.10
  19.5 1.0 %shard_map.51 = (bf16[512,768]{1,0:T(8,128)(2,1)S(1)}, f32[1,512]{1,0:T(1,128)S(1)}, f32[512,512]{1,0:T(8,128)S(1)}, f32[512,1]{1,0:T(8,128)S(1)}, f32[512,1]{1,0:T(8,128)S(1)}, /*index=5*/f32[512,1]{1,0:T(8,128)S(1)}) custom-call(s32[512,1]{1,0:T(8,128)S(1)} %get-tuple-element.30.spot_ref, bf16[512,768]{1,0:T(8,128)(2,1)S(1)} %get-tuple-element.31.q_ref, ...), custom_call_target="tpu_custom_call" | custom-call | flops 512 | bytes 512 | tf_op jit(solution)/shard_map/pallas_call | solution.py:213
  20.5 0.4 %collective-permute-done.10.refs_9_ = bf16[64,768]{1,0:T(8,128)(2,1)S(1)} collective-permute-done((bf16[64,768]{1,0:T(8,128)(2,1)S(1)}, bf16[64,768]{1,0:T(8,128)(2,1)S(1)}, u32[]{:S(2)}, u32[]{:S(2)}) %collective-permute-start.10) | collective-permute-done | bytes 98336 | tf_op jit(solution)/shard_map/ppermute | solution.py:178
  20.9 0.0 collective-permute-done.8.refs_7_
  20.9 0.0 collective-permute-done.9.refs_8_
  20.9 0.0 collective-permute-done.7.refs_6_
  20.9 2.8 %shard_map.52 = (f32[1,512]{1,0:T(1,128)}, bf16[512,768]{1,0:T(8,128)(2,1)}) custom-call(s32[512,1]{1,0:T(8,128)S(1)} %get-tuple-element.30.spot_ref, bf16[512,768]{1,0:T(8,128)(2,1)S(1)} %get-tuple-element.31.q_ref, bf16[512,768]{1,0:T(8,128)(2,1)S(1)} %get-tuple-element.36.refs_0_, f32[1,512]{1,0:T(1,128)S(1)} %get-tuple-element.37.refs_1_, ...), custom_call_target="tpu_custom_call" | custom-call | flops 512 | bytes 512 | tf_op jit(solution)/shard_map/pallas_call | solution.py:246
  (4 shorter events, 0.0 us)
Async XLA Ops:
  0.6 6.9 %copy-start.2 = (bf16[32,768]{1,0:T(8,128)(2,1)S(1)}, bf16[32,768]{1,0:T(8,128)(2,1)}, u32[]{:S(2)}) copy-start(bf16[32,768]{1,0:T(8,128)(2,1)} %param.4) | copy-start | bytes 147460
  0.6 6.9 %collective-permute-start.2 = (bf16[32,768]{1,0:T(8,128)(2,1)}, bf16[32,768]{1,0:T(8,128)(2,1)S(1)}, u32[]{:S(2)}, u32[]{:S(2)}) collective-permute-start(bf16[32,768]{1,0:T(8,128)(2,1)} %param.4), channel_id=1, source_target_pairs={{0,2},{1,3},{2,0},{3,1},{4,6},{5,7},{6,4},{7,5},{8,10},{9,11},{10,... | collective-permute-start | bytes 147464 | tf_op jit(solution)/shard_map/ppermute | solution.py:178
  4.7 6.2 %collective-permute-start.1 = (bf16[32,768]{1,0:T(8,128)(2,1)}, bf16[32,768]{1,0:T(8,128)(2,1)S(1)}, u32[]{:S(2)}, u32[]{:S(2)}) collective-permute-start(bf16[32,768]{1,0:T(8,128)(2,1)} %param.4), channel_id=1, source_target_pairs={{0,3},{1,2},{2,1},{3,0},{4,7},{5,6},{6,5},{7,4},{8,11},{9,10},{10,... | collective-permute-start | bytes 147464 | tf_op jit(solution)/shard_map/ppermute | solution.py:178
  6.1 4.3 %collective-permute-start = (bf16[32,768]{1,0:T(8,128)(2,1)}, bf16[32,768]{1,0:T(8,128)(2,1)S(1)}, u32[]{:S(2)}, u32[]{:S(2)}) collective-permute-start(bf16[32,768]{1,0:T(8,128)(2,1)} %param.4), channel_id=1, source_target_pairs={{0,1},{1,0},{2,3},{3,2},{4,5},{5,4},{6,7},{7,6},{8,9},{9,8},{10,11... | collective-permute-start | bytes 147464 | tf_op jit(solution)/shard_map/ppermute | solution.py:178
  7.6 6.2 %collective-permute-start.3 = (bf16[64,768]{1,0:T(8,128)(2,1)S(1)}, bf16[64,768]{1,0:T(8,128)(2,1)S(1)}, u32[]{:S(2)}, u32[]{:S(2)}) collective-permute-start(bf16[64,768]{1,0:T(8,128)(2,1)S(1)} %pad_maximum_fusion), channel_id=1, source_target_pairs={{0,24},{1,25},{2,26},{3,27},{4,28},{5,29},{6,30},{7,31},{8,16},{9,... | collective-permute-start | bytes 294920 | tf_op jit(solution)/shard_map/ppermute | solution.py:178
  10.9 2.8 %copy-start.1 = (s32[512]{0:T(512)S(1)}, s32[512]{0:T(512)}, u32[]{:S(2)}) copy-start(s32[512]{0:T(512)} %param.5) | copy-start | bytes 6148
  10.9 7.2 %collective-permute-start.5 = (bf16[128,768]{1,0:T(8,128)(2,1)S(1)}, bf16[128,768]{1,0:T(8,128)(2,1)S(1)}, u32[]{:S(2)}, u32[]{:S(2)}) collective-permute-start(bf16[128,768]{1,0:T(8,128)(2,1)S(1)} %constant_dynamic-update-slice_fusion.refs_0_), channel_id=1, source_target_pairs={{0,20},{1,21},{2,22},{3,23},{4,16},{5,17},{6,18},{7,19},{8,28},{9,... | collective-permute-start | bytes 589832 | tf_op jit(solution)/shard_map/ppermute | solution.py:178
  11.0 7.4 %collective-permute-start.4 = (bf16[128,768]{1,0:T(8,128)(2,1)S(1)}, bf16[128,768]{1,0:T(8,128)(2,1)S(1)}, u32[]{:S(2)}, u32[]{:S(2)}) collective-permute-start(bf16[128,768]{1,0:T(8,128)(2,1)S(1)} %constant_dynamic-update-slice_fusion.refs_0_), channel_id=1, source_target_pairs={{0,12},{1,13},{2,14},{3,15},{4,8},{5,9},{6,10},{7,11},{8,4},{9,5},... | collective-permute-start | bytes 589832 | tf_op jit(solution)/shard_map/ppermute | solution.py:178
  13.7 4.4 %collective-permute-start.6 = (bf16[64,768]{1,0:T(8,128)(2,1)S(1)}, bf16[64,768]{1,0:T(8,128)(2,1)S(1)}, u32[]{:S(2)}, u32[]{:S(2)}) collective-permute-start(bf16[64,768]{1,0:T(8,128)(2,1)S(1)} %collective-permute-done.3.refs_1_), channel_id=1, source_target_pairs={{0,5},{1,4},{2,7},{3,6},{4,1},{5,0},{6,3},{7,2},{8,13},{9,12},{10,... | collective-permute-start | bytes 294920 | tf_op jit(solution)/shard_map/ppermute | solution.py:178
  13.7 1.1 %copy-start = (bf16[512,768]{1,0:T(8,128)(2,1)S(1)}, bf16[512,768]{1,0:T(8,128)(2,1)}, u32[]{:S(2)}) copy-start(bf16[512,768]{1,0:T(8,128)(2,1)} %queries_hbm) | copy-start | bytes 2359300
  18.4 2.5 %collective-permute-start.7 = (bf16[192,768]{1,0:T(8,128)(2,1)S(1)}, bf16[192,768]{1,0:T(8,128)(2,1)S(1)}, u32[]{:S(2)}, u32[]{:S(2)}) collective-permute-start(bf16[192,768]{1,0:T(8,128)(2,1)S(1)} %get-tuple-element.32.refs_0_), channel_id=1, source_target_pairs={{0,4},{1,5},{2,6},{3,7},{4,0},{5,1},{6,2},{7,3},{8,12},{9,13},{10,... | collective-permute-start | bytes 884744 | tf_op jit(solution)/shard_map/ppermute | solution.py:178
  19.0 1.9 %collective-permute-start.8 = (bf16[128,768]{1,0:T(8,128)(2,1)S(1)}, bf16[128,768]{1,0:T(8,128)(2,1)S(1)}, u32[]{:S(2)}, u32[]{:S(2)}) collective-permute-start(bf16[128,768]{1,0:T(8,128)(2,1)S(1)} %collective-permute-done.4.refs_1_), channel_id=1, source_target_pairs={{0,4},{1,5},{2,6},{3,7},{4,0},{5,1},{6,2},{7,3},{8,12},{9,13},{10,... | collective-permute-start | bytes 589832 | tf_op jit(solution)/shard_map/ppermute | solution.py:178
  19.0 1.9 %collective-permute-start.9 = (bf16[128,768]{1,0:T(8,128)(2,1)S(1)}, bf16[128,768]{1,0:T(8,128)(2,1)S(1)}, u32[]{:S(2)}, u32[]{:S(2)}) collective-permute-start(bf16[128,768]{1,0:T(8,128)(2,1)S(1)} %collective-permute-done.5.refs_2_), channel_id=1, source_target_pairs={{0,4},{1,5},{2,6},{3,7},{4,0},{5,1},{6,2},{7,3},{8,12},{9,13},{10,... | collective-permute-start | bytes 589832 | tf_op jit(solution)/shard_map/ppermute | solution.py:178
  19.5 1.4 %collective-permute-start.10 = (bf16[64,768]{1,0:T(8,128)(2,1)S(1)}, bf16[64,768]{1,0:T(8,128)(2,1)S(1)}, u32[]{:S(2)}, u32[]{:S(2)}) collective-permute-start(bf16[64,768]{1,0:T(8,128)(2,1)S(1)} %collective-permute-done.6.refs_3_), channel_id=1, source_target_pairs={{0,4},{1,5},{2,6},{3,7},{4,0},{5,1},{6,2},{7,3},{8,12},{9,13},{10,... | collective-permute-start | bytes 294920 | tf_op jit(solution)/shard_map/ppermute | solution.py:178

commit v6 on v5

--- a/solution.py
+++ b/solution.py
@@ -236,10 +236,11 @@
     parts, positives, queries = barrier(([c[0] for c in [column] + firsts], positives, queries))
     spots, loaded, packed = load(positives, queries, parts)
     chunks = [(packed, [p for c in [column] + firsts for p in c[1]])] + chunks
+    early, early_places = swap(chunks[0], 1)
     spots, loaded, arrays = barrier((spots, loaded, [array for array, _ in chunks]))
     chunks = [(array, places) for array, (_, places) in zip(arrays, chunks)]
     middle = score(spots, loaded, chunks)
-    mirrored = [swap(chunk, 1) for chunk in chunks]
+    mirrored = [(early, early_places)] + [swap(chunk, 1) for chunk in chunks[1:]]
     docs = own * narrow * wide
     bases = [bases_of(chunks), bases_of(mirrored)]
     n_late = len(bases[-1]) * own

time: 24 us -> 23.7 us (0.987)
  waiting for transfers between devices: 4.67 us -> 2.03 us
  starting transfers between devices: 12.3 us -> 14.6 us
    ppermute x11, waiting for transfers between devices: 4.67 us -> 2.03 us  [swap(): lax.ppermute(array, AXES, pairs)]
    ppermute x11, starting transfers between devices: 12.3 us -> 14.6 us  [swap(): lax.ppermute(array, AXES, pairs)]
where the time goes in v6:
time: 23.7 us; the launch traced here: 23.4 us
  starting transfers between devices  14.6 us (62%)
  Pallas kernels  4.09 us (17%)
  waiting for transfers between devices  2.03 us (9%)
  local copies, waits for them, and re-layouts  1.98 us (8%)
  between operations  0.69 us (3%)
    ppermute x11, starting transfers between devices, swap(): lax.ppermute(array, AXES, pairs)  14.6 us
    pallas_call x1, Pallas kernels, shards(): pl.pallas_call(functools.partial(late_kernel, bases, own, block), out_sha...  2.83 us
    ppermute x11, waiting for transfers between devices, swap(): lax.ppermute(array, AXES, pairs)  2.03 us
    unnamed x9, local copies, waits for them, and re-layouts  1.98 us
    pallas_call x1, Pallas kernels, score(): pl.pallas_call(functools.partial(early_kernel, bases, own, block), out_sh...  1.01 us
  transfers between devices with their start and end apart: 11, of which 6 were waited for; matrix products, arithmetic and copies ran while one was open for 4% of the time, Pallas kernels for 5%

profile of v6, /device:TPU:0, one launch (start us, length us, event | category | flops | bytes accessed | tf_op | source)
XLA Modules:
  0.0 23.4 jit_solution(13093469876395117246)
XLA Ops:
  0.6 0.0 copy-start.2
  0.6 4.1 %collective-permute-start.2 = (bf16[32,768]{1,0:T(8,128)(2,1)}, bf16[32,768]{1,0:T(8,128)(2,1)S(1)}, u32[]{:S(2)}, u32[]{:S(2)}) collective-permute-start(bf16[32,768]{1,0:T(8,128)(2,1)} %param.4), channel_id=1, source_target_pairs={{0,2},{1,3},{2,0},{3,1},{4,6},{5,7},{6,4},{7,5},{8,10},{9,11},{10,... | collective-permute-start | bytes 147464 | tf_op jit(solution)/shard_map/ppermute | solution.py:178
  4.7 1.3 %collective-permute-start.1 = (bf16[32,768]{1,0:T(8,128)(2,1)}, bf16[32,768]{1,0:T(8,128)(2,1)S(1)}, u32[]{:S(2)}, u32[]{:S(2)}) collective-permute-start(bf16[32,768]{1,0:T(8,128)(2,1)} %param.4), channel_id=1, source_target_pairs={{0,3},{1,2},{2,1},{3,0},{4,7},{5,6},{6,5},{7,4},{8,11},{9,10},{10,... | collective-permute-start | bytes 147464 | tf_op jit(solution)/shard_map/ppermute | solution.py:178
  6.1 0.2 collective-permute-start
  6.3 0.8 %constant_dynamic-update-slice_fusion.3 = bf16[128,768]{1,0:T(8,128)(2,1)S(1)} fusion(bf16[32,768]{1,0:T(8,128)(2,1)} %param.4), kind=kLoop, calls=%fused_computation.4 | loop fusion | bytes 98304
  7.2 0.4 %collective-permute-done.2 = bf16[32,768]{1,0:T(8,128)(2,1)S(1)} collective-permute-done((bf16[32,768]{1,0:T(8,128)(2,1)}, bf16[32,768]{1,0:T(8,128)(2,1)S(1)}, u32[]{:S(2)}, u32[]{:S(2)}) %collective-permute-start.2) | collective-permute-done | bytes 49184 | tf_op jit(solution)/shard_map/ppermute | solution.py:178
  7.5 0.0 copy-done.2
  7.6 2.7 %collective-permute-start.3 = (bf16[64,768]{1,0:T(8,128)(2,1)S(1)}, bf16[64,768]{1,0:T(8,128)(2,1)S(1)}, u32[]{:S(2)}, u32[]{:S(2)}) collective-permute-start(bf16[64,768]{1,0:T(8,128)(2,1)S(1)} %pad_maximum_fusion), channel_id=1, source_target_pairs={{0,24},{1,25},{2,26},{3,27},{4,28},{5,29},{6,30},{7,31},{8,16},{9,... | collective-permute-start | bytes 294920 | tf_op jit(solution)/shard_map/ppermute | solution.py:178
  10.3 0.1 collective-permute-done
  10.4 0.5 %collective-permute-done.1 = bf16[32,768]{1,0:T(8,128)(2,1)S(1)} collective-permute-done((bf16[32,768]{1,0:T(8,128)(2,1)}, bf16[32,768]{1,0:T(8,128)(2,1)S(1)}, u32[]{:S(2)}, u32[]{:S(2)}) %collective-permute-start.1) | collective-permute-done | bytes 49184 | tf_op jit(solution)/shard_map/ppermute | solution.py:178
  10.9 0.0 copy-start.1
  10.9 0.1 collective-permute-start.5
  11.0 2.7 %collective-permute-start.4 = (bf16[128,768]{1,0:T(8,128)(2,1)S(1)}, bf16[128,768]{1,0:T(8,128)(2,1)S(1)}, u32[]{:S(2)}, u32[]{:S(2)}) collective-permute-start(bf16[128,768]{1,0:T(8,128)(2,1)S(1)} %constant_dynamic-update-slice_fusion.refs_0_), channel_id=1, source_target_pairs={{0,12},{1,13},{2,14},{3,15},{4,8},{5,9},{6,10},{7,11},{8,4},{9,5},... | collective-permute-start | bytes 589832 | tf_op jit(solution)/shard_map/ppermute | solution.py:178
  13.7 0.0 collective-permute-done.3.refs_1_
  13.7 0.0 collective-permute-start.6
  13.7 0.0 copy-done.1
  13.7 0.0 copy-start
  13.8 1.1 %copy-done = bf16[512,768]{1,0:T(8,128)(2,1)S(1)} copy-done((bf16[512,768]{1,0:T(8,128)(2,1)S(1)}, bf16[512,768]{1,0:T(8,128)(2,1)}, u32[]{:S(2)}) %copy-start) | copy-done | bytes 786456
  14.9 0.2 %shard_map.50 = (s32[512,1]{1,0:T(8,128)S(1)}, bf16[512,768]{1,0:T(8,128)(2,1)S(1)}, bf16[192,768]{1,0:T(8,128)(2,1)S(1)}) custom-call(s32[1,512]{1,0:T(1,128)S(1)} %bitcast.2, bf16[512,768]{1,0:T(8,128)(2,1)S(1)} %copy-done, bf16[128,768]{1,0:T(8,128)(2,1)S(1)} %constant_dynamic-update-slice_fusion.refs_0_, bf16[64,768]{1,0:T(8,128)(2,1)S(1)} %collective-permute-done.3.refs_1_), custom_call_target="tpu_custom_call" | custom-call | flops 512 | bytes 512 | tf_op jit(solution)/shard_map/pallas_call | solution.py:193
  15.1 2.3 %collective-permute-start.7 = (bf16[192,768]{1,0:T(8,128)(2,1)S(1)}, bf16[192,768]{1,0:T(8,128)(2,1)S(1)}, u32[]{:S(2)}, u32[]{:S(2)}) collective-permute-start(bf16[192,768]{1,0:T(8,128)(2,1)S(1)} %get-tuple-element.32.refs_0_), channel_id=1, source_target_pairs={{0,4},{1,5},{2,6},{3,7},{4,0},{5,1},{6,2},{7,3},{8,12},{9,13},{10,... | collective-permute-start | bytes 884744 | tf_op jit(solution)/shard_map/ppermute | solution.py:178
  17.4 0.7 %collective-permute-done.6.refs_3_ = bf16[64,768]{1,0:T(8,128)(2,1)S(1)} collective-permute-done((bf16[64,768]{1,0:T(8,128)(2,1)S(1)}, bf16[64,768]{1,0:T(8,128)(2,1)S(1)}, u32[]{:S(2)}, u32[]{:S(2)}) %collective-permute-start.6) | collective-permute-done | bytes 98336 | tf_op jit(solution)/shard_map/ppermute | solution.py:178
  18.2 0.0 collective-permute-done.5.refs_2_
  18.2 0.2 collective-permute-done.4.refs_1_
  18.4 0.6 %collective-permute-start.8 = (bf16[128,768]{1,0:T(8,128)(2,1)S(1)}, bf16[128,768]{1,0:T(8,128)(2,1)S(1)}, u32[]{:S(2)}, u32[]{:S(2)}) collective-permute-start(bf16[128,768]{1,0:T(8,128)(2,1)S(1)} %collective-permute-done.4.refs_1_), channel_id=1, source_target_pairs={{0,4},{1,5},{2,6},{3,7},{4,0},{5,1},{6,2},{7,3},{8,12},{9,13},{10,... | collective-permute-start | bytes 589832 | tf_op jit(solution)/shard_map/ppermute | solution.py:178
  19.0 0.0 collective-permute-start.9
  19.0 0.5 %collective-permute-start.10 = (bf16[64,768]{1,0:T(8,128)(2,1)S(1)}, bf16[64,768]{1,0:T(8,128)(2,1)S(1)}, u32[]{:S(2)}, u32[]{:S(2)}) collective-permute-start(bf16[64,768]{1,0:T(8,128)(2,1)S(1)} %collective-permute-done.6.refs_3_), channel_id=1, source_target_pairs={{0,4},{1,5},{2,6},{3,7},{4,0},{5,1},{6,2},{7,3},{8,12},{9,13},{10,... | collective-permute-start | bytes 294920 | tf_op jit(solution)/shard_map/ppermute | solution.py:178
  19.5 1.0 %shard_map.51 = (bf16[512,768]{1,0:T(8,128)(2,1)S(1)}, f32[1,512]{1,0:T(1,128)S(1)}, f32[512,512]{1,0:T(8,128)S(1)}, f32[512,1]{1,0:T(8,128)S(1)}, f32[512,1]{1,0:T(8,128)S(1)}, /*index=5*/f32[512,1]{1,0:T(8,128)S(1)}) custom-call(s32[512,1]{1,0:T(8,128)S(1)} %get-tuple-element.30.spot_ref, bf16[512,768]{1,0:T(8,128)(2,1)S(1)} %get-tuple-element.31.q_ref, ...), custom_call_target="tpu_custom_call" | custom-call | flops 512 | bytes 512 | tf_op jit(solution)/shard_map/pallas_call | solution.py:213
  20.5 0.1 collective-permute-done.10.refs_9_
  20.6 0.0 collective-permute-done.8.refs_7_
  20.6 0.0 collective-permute-done.9.refs_8_
  20.6 0.0 collective-permute-done.7.refs_6_
  20.6 2.8 %shard_map.52 = (f32[1,512]{1,0:T(1,128)}, bf16[512,768]{1,0:T(8,128)(2,1)}) custom-call(s32[512,1]{1,0:T(8,128)S(1)} %get-tuple-element.30.spot_ref, bf16[512,768]{1,0:T(8,128)(2,1)S(1)} %get-tuple-element.31.q_ref, bf16[512,768]{1,0:T(8,128)(2,1)S(1)} %get-tuple-element.36.refs_0_, f32[1,512]{1,0:T(1,128)S(1)} %get-tuple-element.37.refs_1_, ...), custom_call_target="tpu_custom_call" | custom-call | flops 512 | bytes 512 | tf_op jit(solution)/shard_map/pallas_call | solution.py:247
  (4 shorter events, 0.0 us)
Async XLA Ops:
  0.6 6.9 %copy-start.2 = (bf16[32,768]{1,0:T(8,128)(2,1)S(1)}, bf16[32,768]{1,0:T(8,128)(2,1)}, u32[]{:S(2)}) copy-start(bf16[32,768]{1,0:T(8,128)(2,1)} %param.4) | copy-start | bytes 147460
  0.6 6.9 %collective-permute-start.2 = (bf16[32,768]{1,0:T(8,128)(2,1)}, bf16[32,768]{1,0:T(8,128)(2,1)S(1)}, u32[]{:S(2)}, u32[]{:S(2)}) collective-permute-start(bf16[32,768]{1,0:T(8,128)(2,1)} %param.4), channel_id=1, source_target_pairs={{0,2},{1,3},{2,0},{3,1},{4,6},{5,7},{6,4},{7,5},{8,10},{9,11},{10,... | collective-permute-start | bytes 147464 | tf_op jit(solution)/shard_map/ppermute | solution.py:178
  4.7 6.2 %collective-permute-start.1 = (bf16[32,768]{1,0:T(8,128)(2,1)}, bf16[32,768]{1,0:T(8,128)(2,1)S(1)}, u32[]{:S(2)}, u32[]{:S(2)}) collective-permute-start(bf16[32,768]{1,0:T(8,128)(2,1)} %param.4), channel_id=1, source_target_pairs={{0,3},{1,2},{2,1},{3,0},{4,7},{5,6},{6,5},{7,4},{8,11},{9,10},{10,... | collective-permute-start | bytes 147464 | tf_op jit(solution)/shard_map/ppermute | solution.py:178
  6.1 4.3 %collective-permute-start = (bf16[32,768]{1,0:T(8,128)(2,1)}, bf16[32,768]{1,0:T(8,128)(2,1)S(1)}, u32[]{:S(2)}, u32[]{:S(2)}) collective-permute-start(bf16[32,768]{1,0:T(8,128)(2,1)} %param.4), channel_id=1, source_target_pairs={{0,1},{1,0},{2,3},{3,2},{4,5},{5,4},{6,7},{7,6},{8,9},{9,8},{10,11... | collective-permute-start | bytes 147464 | tf_op jit(solution)/shard_map/ppermute | solution.py:178
  7.6 6.2 %collective-permute-start.3 = (bf16[64,768]{1,0:T(8,128)(2,1)S(1)}, bf16[64,768]{1,0:T(8,128)(2,1)S(1)}, u32[]{:S(2)}, u32[]{:S(2)}) collective-permute-start(bf16[64,768]{1,0:T(8,128)(2,1)S(1)} %pad_maximum_fusion), channel_id=1, source_target_pairs={{0,24},{1,25},{2,26},{3,27},{4,28},{5,29},{6,30},{7,31},{8,16},{9,... | collective-permute-start | bytes 294920 | tf_op jit(solution)/shard_map/ppermute | solution.py:178
  10.9 2.8 %copy-start.1 = (s32[512]{0:T(512)S(1)}, s32[512]{0:T(512)}, u32[]{:S(2)}) copy-start(s32[512]{0:T(512)} %param.5) | copy-start | bytes 6148
  10.9 7.2 %collective-permute-start.5 = (bf16[128,768]{1,0:T(8,128)(2,1)S(1)}, bf16[128,768]{1,0:T(8,128)(2,1)S(1)}, u32[]{:S(2)}, u32[]{:S(2)}) collective-permute-start(bf16[128,768]{1,0:T(8,128)(2,1)S(1)} %constant_dynamic-update-slice_fusion.refs_0_), channel_id=1, source_target_pairs={{0,20},{1,21},{2,22},{3,23},{4,16},{5,17},{6,18},{7,19},{8,28},{9,... | collective-permute-start | bytes 589832 | tf_op jit(solution)/shard_map/ppermute | solution.py:178
  11.0 7.4 %collective-permute-start.4 = (bf16[128,768]{1,0:T(8,128)(2,1)S(1)}, bf16[128,768]{1,0:T(8,128)(2,1)S(1)}, u32[]{:S(2)}, u32[]{:S(2)}) collective-permute-start(bf16[128,768]{1,0:T(8,128)(2,1)S(1)} %constant_dynamic-update-slice_fusion.refs_0_), channel_id=1, source_target_pairs={{0,12},{1,13},{2,14},{3,15},{4,8},{5,9},{6,10},{7,11},{8,4},{9,5},... | collective-permute-start | bytes 589832 | tf_op jit(solution)/shard_map/ppermute | solution.py:178
  13.7 4.4 %collective-permute-start.6 = (bf16[64,768]{1,0:T(8,128)(2,1)S(1)}, bf16[64,768]{1,0:T(8,128)(2,1)S(1)}, u32[]{:S(2)}, u32[]{:S(2)}) collective-permute-start(bf16[64,768]{1,0:T(8,128)(2,1)S(1)} %collective-permute-done.3.refs_1_), channel_id=1, source_target_pairs={{0,5},{1,4},{2,7},{3,6},{4,1},{5,0},{6,3},{7,2},{8,13},{9,12},{10,... | collective-permute-start | bytes 294920 | tf_op jit(solution)/shard_map/ppermute | solution.py:178
  13.7 1.1 %copy-start = (bf16[512,768]{1,0:T(8,128)(2,1)S(1)}, bf16[512,768]{1,0:T(8,128)(2,1)}, u32[]{:S(2)}) copy-start(bf16[512,768]{1,0:T(8,128)(2,1)} %queries_hbm) | copy-start | bytes 2359300
  15.1 5.5 %collective-permute-start.7 = (bf16[192,768]{1,0:T(8,128)(2,1)S(1)}, bf16[192,768]{1,0:T(8,128)(2,1)S(1)}, u32[]{:S(2)}, u32[]{:S(2)}) collective-permute-start(bf16[192,768]{1,0:T(8,128)(2,1)S(1)} %get-tuple-element.32.refs_0_), channel_id=1, source_target_pairs={{0,4},{1,5},{2,6},{3,7},{4,0},{5,1},{6,2},{7,3},{8,12},{9,13},{10,... | collective-permute-start | bytes 884744 | tf_op jit(solution)/shard_map/ppermute | solution.py:178
  18.4 2.2 %collective-permute-start.8 = (bf16[128,768]{1,0:T(8,128)(2,1)S(1)}, bf16[128,768]{1,0:T(8,128)(2,1)S(1)}, u32[]{:S(2)}, u32[]{:S(2)}) collective-permute-start(bf16[128,768]{1,0:T(8,128)(2,1)S(1)} %collective-permute-done.4.refs_1_), channel_id=1, source_target_pairs={{0,4},{1,5},{2,6},{3,7},{4,0},{5,1},{6,2},{7,3},{8,12},{9,13},{10,... | collective-permute-start | bytes 589832 | tf_op jit(solution)/shard_map/ppermute | solution.py:178
  19.0 1.6 %collective-permute-start.9 = (bf16[128,768]{1,0:T(8,128)(2,1)S(1)}, bf16[128,768]{1,0:T(8,128)(2,1)S(1)}, u32[]{:S(2)}, u32[]{:S(2)}) collective-permute-start(bf16[128,768]{1,0:T(8,128)(2,1)S(1)} %collective-permute-done.5.refs_2_), channel_id=1, source_target_pairs={{0,4},{1,5},{2,6},{3,7},{4,0},{5,1},{6,2},{7,3},{8,12},{9,13},{10,... | collective-permute-start | bytes 589832 | tf_op jit(solution)/shard_map/ppermute | solution.py:178
  19.0 1.6 %collective-permute-start.10 = (bf16[64,768]{1,0:T(8,128)(2,1)S(1)}, bf16[64,768]{1,0:T(8,128)(2,1)S(1)}, u32[]{:S(2)}, u32[]{:S(2)}) collective-permute-start(bf16[64,768]{1,0:T(8,128)(2,1)S(1)} %collective-permute-done.6.refs_3_), channel_id=1, source_target_pairs={{0,4},{1,5},{2,6},{3,7},{4,0},{5,1},{6,2},{7,3},{8,12},{9,13},{10,... | collective-permute-start | bytes 294920 | tf_op jit(solution)/shard_map/ppermute | solution.py:178
